TPU v7x, 768 devices: a whole 4x8x12 slice. The times are simulated.
768 devices in a mesh: rep: 16 (over y, core), row: 48 (over x, z).
Axes of the slice: x: 4, y: 8, z: 12, core: 2. Of those that a mesh axis runs over, the one named last changes fastest.
Arguments:
- dense_act: bfloat16 [393216, 256], P(('rep', 'row')), may hold values from -6 to 6
- upstream: bfloat16 [393216, 1024], P(('rep', 'row')), may hold values from -6 to 6
- bottom_weight: bfloat16 [256, 128], replicated, may hold values from -0.375 to 0.375
- top_weight: bfloat16 [384, 1024], replicated, may hold values from -0.3125 to 0.3125
- hot_table: bfloat16 [512, 128], replicated, may hold values from -3 to 3
- cold_table: bfloat16 [196608, 128], P('row'), may hold values from -3 to 3
- hot_bags: int32 [393216, 8], P(('rep', 'row')), may hold values from 0 to 511
- cold_bags: int32 [393216, 16], P(('rep', 'row')), may hold values from 0 to 3071
- requests: int32 [16, 48, 48, 64], P('rep', 'row'), may hold values from 0 to 4095
Outputs:
- top_grad: float32 [384, 1024], replicated
- bottom_grad: float32 [256, 128], replicated
- hot_grad: float32 [512, 128], replicated
- cold_grad: float32 [196608, 128], P('row')
All inputs are finite; a program needn't handle non-finite values.
Results may differ from a plain program's by a relative error of at most 0.015.
Values may be sent and summed in bfloat16 or wider, within the bound.
A program may use at most 32 MiB of HBM per device.

v0:
```python
import jax
import jax.numpy as jnp
from jax import lax
from jax.sharding import PartitionSpec as P


def silu_slope(value):
    sigma = jax.nn.sigmoid(value)
    return sigma * (1.0 + value * (1.0 - sigma))


def local(
    dense_act,
    upstream,
    bottom_weight,
    top_weight,
    hot_table,
    cold_table,
    hot_bags,
    cold_bags,
    requests,
):
    row_count = requests.shape[2]
    slot_cap = requests.shape[3]
    width = cold_table.shape[1]
    owned_rows = cold_table.shape[0]
    batch_rows = dense_act.shape[0]
    cold_reads = cold_bags.shape[1]
    hot_reads = hot_bags.shape[1]
    hot_rows = hot_table.shape[0]
    asked = requests.reshape(row_count, slot_cap)
    shard_ids = lax.all_to_all(asked, "row", split_axis=0, concat_axis=0, tiled=True)
    gathered = cold_table[shard_ids]
    returned = lax.all_to_all(gathered, "row", split_axis=0, concat_axis=0, tiled=True)
    fetched = returned
    fetched = fetched.reshape(row_count * slot_cap, width)
    bottom_pre = jnp.dot(dense_act, bottom_weight, preferred_element_type=jnp.float32)
    lower = jax.nn.silu(bottom_pre)
    cold_pool = jnp.sum(fetched[cold_bags].astype(jnp.float32), axis=1)
    hot_pool = jnp.sum(hot_table[hot_bags].astype(jnp.float32), axis=1)
    features = jnp.concatenate([lower, cold_pool, hot_pool], axis=1).astype(jnp.bfloat16)
    top_pre = jnp.dot(features, top_weight, preferred_element_type=jnp.float32)
    top_delta = (upstream.astype(jnp.float32) * silu_slope(top_pre)).astype(jnp.bfloat16)
    top_local = jnp.dot(features.T, top_delta, preferred_element_type=jnp.float32)
    feature_grad = jnp.dot(top_delta, top_weight.T, preferred_element_type=jnp.float32)
    lower_grad = feature_grad[:, :width]
    cold_back = feature_grad[:, width : 2 * width]
    hot_back = feature_grad[:, 2 * width :]
    bottom_delta = (lower_grad * silu_slope(bottom_pre)).astype(jnp.bfloat16)
    bottom_local = jnp.dot(dense_act.T, bottom_delta, preferred_element_type=jnp.float32)
    hot_terms = jnp.broadcast_to(hot_back[:, None, :], (batch_rows, hot_reads, width)).reshape(
        -1, width
    )
    hot_local = jax.ops.segment_sum(hot_terms, hot_bags.reshape(-1), num_segments=hot_rows)
    cold_terms = jnp.broadcast_to(cold_back[:, None, :], (batch_rows, cold_reads, width)).reshape(
        -1, width
    )
    slot_grad = jax.ops.segment_sum(
        cold_terms, cold_bags.reshape(-1), num_segments=row_count * slot_cap
    )
    slot_grad = slot_grad.astype(jnp.bfloat16).reshape(row_count, slot_cap, width)
    arrived = lax.all_to_all(slot_grad, "row", split_axis=0, concat_axis=0, tiled=True)
    owner_grad = jax.ops.segment_sum(
        arrived.reshape(-1, width).astype(jnp.float32),
        shard_ids.reshape(-1),
        num_segments=owned_rows,
    )
    cold_grad = lax.psum(owner_grad.astype(jnp.bfloat16), "rep").astype(jnp.float32)
    top_grad, bottom_grad, hot_grad = lax.psum((top_local, bottom_local, hot_local), ("rep", "row"))
    return (top_grad, bottom_grad, hot_grad, cold_grad)


def solution(mesh):
    placed = (
        P(("rep", "row"), None),
        P(("rep", "row"), None),
        P(),
        P(),
        P(),
        P("row", None),
        P(("rep", "row"), None),
        P(("rep", "row"), None),
        P("rep", "row", None, None),
    )
    return jax.shard_map(
        local,
        mesh=mesh,
        in_specs=placed,
        out_specs=(P(), P(), P(), P("row", None)),
        check_vma=False,
    )
```

profile of v0, /device:TPU:1, one launch (start us, length us, event | category | flops | bytes accessed | tf_op | source)
XLA Modules:
  0.0 834.6 jit_solution(5738486665727555576)
XLA Ops:
  7.2 0.0 copy-start
  7.2 30.0 %all_to_all.22 = s32[48,1,64]{2,1,0:T(1,128)S(1)} all-to-all(s32[48,1,64]{2,1,0:T(1,128)} %bitcast.31), channel_id=1, replica_groups=mesh['rep'=16,'row'=48] {'row'}, dimensions={0} | all-to-all | bytes 24576 | tf_op jit(solution)/shard_map/all_to_all | solution.py:32
  37.2 0.6 copy-done.10
  37.8 0.1 reshape.65
  37.9 0.0 copy-done
  37.9 0.0 copy-start.13
  37.9 11.5 %gather_fusion = bf16[3072,128]{1,0:T(8,128)(2,1)} fusion(bf16[4096,128]{1,0:T(8,128)(2,1)S(1)} %copy-done, s32[3072]{0:T(1024)S(1)} %broadcast_clamp_fusion.2), kind=kCustom, calls=%fused_computation | custom fusion | bytes 1585152 | tf_op jit(solution)/shard_map/gather | solution.py:33
  49.5 4.7 all-to-all-start.1
  54.2 0.0 copy-done.13
  54.2 0.1 copy.27
  54.3 0.1 copy.21
  54.5 0.1 reshape.73
  54.6 0.0 copy-done.14
  54.6 0.1 copy.22
  54.7 0.2 reshape.81
  54.9 0.1 reshape.97
  55.0 0.0 copy-done.1
  55.1 0.0 copy-start.15
  55.1 12.1 %gather_fusion.2 = bf16[4096,128]{1,0:T(8,128)(2,1)S(1)} fusion(bf16[512,128]{1,0:T(8,128)(2,1)S(1)} %copy-done.1, s32[4096]{0:T(1024)S(1)} %broadcast_clamp_fusion.1), kind=kCustom, calls=%fused_computation.2 | custom fusion | bytes 2113536 | tf_op jit(solution)/shard_map/gather | solution.py:40
  67.2 0.7 bitcast_reduce_fusion.1
  67.9 0.1 copy.24
  68.0 0.0 copy-done.15
  68.1 1.8 multiply_convert_fusion.2
  69.8 12.8 %all-to-all-done.1 = bf16[48,64,128]{2,1,0:T(8,128)(2,1)S(1)} async-done(((bf16[48,64,128]{2,1,0:T(8,128)(2,1)}), bf16[48,64,128]{2,1,0:T(8,128)(2,1)S(1)}, u32[]{:S(2)}, u32[]{:S(2)}) %all-to-all-start.1) | async-done | bytes 786464 | tf_op jit(solution)/shard_map/all_to_all | solution.py:34
  82.6 29.5 %gather_fusion.1 = bf16[8192,128]{1,0:T(8,128)(2,1)} fusion(bf16[3072,128]{1,0:T(8,128)(2,1)S(1)} %bitcast.26, s32[8192]{0:T(1024)S(1)} %broadcast_clamp_fusion), kind=kCustom, calls=%fused_computation.1 | custom fusion | bytes 4227072 | tf_op jit(solution)/shard_map/gather | solution.py:39
  112.1 2.7 bitcast_reduce_fusion
  114.8 0.1 copy.23
  114.9 0.0 copy-start.7
  114.9 0.0 copy-done.12
  114.9 0.0 copy-done.6
  114.9 2.5 multiply_convert_fusion
  117.5 0.0 copy-done.7
  117.5 0.0 copy-start.2
  117.5 0.7 fusion.15
  118.2 0.8 fusion.14
  119.0 0.0 copy-done.2
  119.0 2.2 broadcast_in_dim.34
  121.2 44.7 %scatter_custom_fusion.1 = f32[3072,128]{1,0:T(8,128)S(1)} fusion(s32[8192]{0:T(1024)S(1)} %reshape.97, f32[8192,128]{1,0:T(8,128)} %bitcast.27, f32[]{:T(128)} %constant.10.clone.1), kind=kCustom, calls=%fused_computation.16 | custom fusion | flops 1048576 | bytes 1573376 | tf_op jit(solution)/shard_map/scatter-add | solution.py:58
  165.9 1.0 convert_element_type.36
  166.9 11.6 %all-to-all-start.2 = ((bf16[48,64,128]{2,1,0:T(8,128)(2,1)}), bf16[48,64,128]{2,1,0:T(8,128)(2,1)S(1)}, u32[]{:S(2)}, u32[]{:S(2)}) async-start(bf16[48,64,128]{2,1,0:T(8,128)(2,1)} %bitcast.29), calls=%async_computation.2 | async-start | bytes 1572864 | tf_op jit(solution)/shard_map/all_to_all | solution.py:62
  178.5 0.2 all-reduce.6.cloned.1.call-start
  178.7 0.1 copy.26
  178.8 0.2 reshape.89
  179.0 0.0 copy-start.8
  179.0 1.8 copy.29
  180.9 23.0 %scatter_custom_fusion = f32[512,128]{1,0:T(8,128)} fusion(s32[4096]{0:T(1024)S(1)} %reshape.89, f32[512,128]{1,0:T(8,128)S(1)} %get-tuple-element.20, f32[]{:T(128)} %constant.10.clone.1), kind=kCustom, calls=%fused_computation.6 | custom fusion | flops 524288 | bytes 524292 | tf_op jit(solution)/shard_map/scatter-add | solution.py:54
  203.9 2.0 convolution_bitcast_fusion
  205.9 2.6 fusion.8
  208.5 0.0 all-reduce.6.cloned.1.call-update
  208.6 0.0 all-reduce.4.cloned.1.call-start
  208.6 0.5 broadcast.39
  209.1 0.7 reduce.9
  209.8 0.1 reshape.105
  209.9 0.0 all-to-all-done.2
  209.9 0.9 copy-done.4
  210.8 17.8 %scatter_custom_fusion.2 = f32[4096,128]{1,0:T(8,128)S(1)} fusion(s32[3072]{0:T(1024)S(1)} %reshape.105, bf16[3072,128]{1,0:T(8,128)(2,1)} %bitcast.28, f32[]{:T(128)} %constant.10.clone.1), kind=kCustom, calls=%fused_computation.10 | custom fusion | flops 786432 | bytes 2883588 | tf_op jit(solution)/shard_map/scatter-add | solution.py:63
  228.6 1.1 convert_element_type.39
  229.7 0.0 all-reduce.4.cloned.1.call-update
  229.7 469.0 %all-reduce.6.cloned.1.call-done = (f32[384,1024]{1,0:T(8,128)}, f32[256,128]{0,1:T(8,128)}, f32[512,128]{1,0:T(8,128)}) async-done(((f32[384,1024]{1,0:T(8,128)}, f32[256,128]{0,1:T(8,128)}, f32[512,128]{1,0:T(8,128)}), (f32[384,1024]{1,0:T(8,128)}, f32[256,128]{0,1:T(8,128)}, f32[512,128]{1,0:T(8,128)})) %all-reduce.6.cloned.1.call-update) | async-done | bytes 1966096 | tf_op jit(solution)/shard_map/psum | solution.py:69
  698.7 1.8 copy.28
  700.5 122.7 %all-reduce.4.cloned.1.call-done = bf16[4096,128]{1,0:T(8,128)(2,1)} async-done(((bf16[4096,128]{1,0:T(8,128)(2,1)}), bf16[4096,128]{1,0:T(8,128)(2,1)}) %all-reduce.4.cloned.1.call-update) | async-done | bytes 1048592 | tf_op jit(solution)/shard_map/psum | solution.py:68
  823.2 2.7 convert_element_type.40
  825.9 1.1 copy.34
  827.0 0.7 copy.35
  (21 shorter events, 0.1 us)
Async XLA Ops:
  7.2 30.7 %copy-start = (bf16[4096,128]{1,0:T(8,128)(2,1)S(1)}, bf16[4096,128]{1,0:T(8,128)(2,1)}, u32[]{:S(2)}) copy-start(bf16[4096,128]{1,0:T(8,128)(2,1)} %param.14) | copy-start | bytes 3145732
  37.2 0.6 copy-start.10
  37.9 16.3 %copy-start.13 = (s32[512,16]{0,1:T(8,128)S(1)}, s32[512,16]{0,1:T(8,128)}, u32[]{:S(2)}) copy-start(s32[512,16]{0,1:T(8,128)} %param.16) | copy-start | bytes 98308
  49.5 5.1 copy-start.14
  49.5 5.6 copy-start.1
  49.5 33.1 %all-to-all-start.1 = ((bf16[48,64,128]{2,1,0:T(8,128)(2,1)}), bf16[48,64,128]{2,1,0:T(8,128)(2,1)S(1)}, u32[]{:S(2)}, u32[]{:S(2)}) async-start(bf16[48,64,128]{2,1,0:T(8,128)(2,1)} %bitcast.2), calls=%async_computation.1 | async-start | bytes 1572864 | tf_op jit(solution)/shard_map/all_to_all | solution.py:34
  55.1 13.0 %copy-start.15 = (bf16[512,256]{1,0:T(8,128)(2,1)S(1)}, bf16[512,256]{1,0:T(8,128)(2,1)}, u32[]{:S(2)}) copy-start(bf16[512,256]{1,0:T(8,128)(2,1)} %param.9) | copy-start | bytes 786436
  69.8 45.1 %copy-start.12 = (bf16[512,128]{0,1:T(8,128)(2,1)}, bf16[512,128]{0,1:T(8,128)(2,1)S(1)}, u32[]{:S(2)}) copy-start(bf16[512,128]{0,1:T(8,128)(2,1)S(1)} %get-tuple-element.22) | copy-start | bytes 393220
  112.1 2.8 copy-start.6
  114.9 2.6 copy-start.7
  117.5 1.5 copy-start.2
  166.9 39.0 %copy-start.3 = (bf16[512,1024]{1,0:T(8,128)(2,1)S(1)}, bf16[512,1024]{1,0:T(8,128)(2,1)}, u32[]{:S(2)}) copy-start(bf16[512,1024]{1,0:T(8,128)(2,1)} %copy-done.2) | copy-start | bytes 3145732
  166.9 43.0 %all-to-all-start.2 = ((bf16[48,64,128]{2,1,0:T(8,128)(2,1)}), bf16[48,64,128]{2,1,0:T(8,128)(2,1)S(1)}, u32[]{:S(2)}, u32[]{:S(2)}) async-start(bf16[48,64,128]{2,1,0:T(8,128)(2,1)} %bitcast.29), calls=%async_computation.2 | async-start | bytes 1572864 | tf_op jit(solution)/shard_map/all_to_all | solution.py:62
  178.5 520.2 %all-reduce.6.cloned.1.call-start = ((), (), s32[]{:S(2)}) async-start(), calls=%async_computation.4 | async-start | bytes 3932160 | tf_op jit(solution)/shard_map/psum | solution.py:69
  179.0 26.9 %copy-start.8 = (bf16[512,128]{0,1:T(8,128)(2,1)S(1)}, bf16[512,128]{0,1:T(8,128)(2,1)}, u32[]{:S(2)}) copy-start(bf16[512,128]{0,1:T(8,128)(2,1)} %copy-done.7) | copy-start | bytes 393220
  205.9 3.2 copy-start.11
  208.6 614.6 %all-reduce.4.cloned.1.call-start = ((), (), s32[]{:S(2)}) async-start(), calls=%async_computation.3 | async-start | bytes 2097152 | tf_op jit(solution)/shard_map/psum | solution.py:68
  209.9 0.9 copy-start.4
  698.7 127.2 %copy-start.5 = (f32[384,1024]{1,0:T(8,128)S(1)}, f32[384,1024]{1,0:T(8,128)}, u32[]{:S(2)}) copy-start(f32[384,1024]{1,0:T(8,128)} %get-tuple-element.24) | copy-start | bytes 4718596
  825.9 1.1 copy-start.9
Sparse Core Ops, SparseCore 0:
  208.7 489.9 all-reduce.5
  701.6 121.5 all-reduce.3
where the time goes:
time: 835 us
  waiting for transfers between devices  605 us (72%)
  other arithmetic  94.4 us (11%)
  local copies, waits for them, and re-layouts  65.1 us (8%)
  blocking collectives  30 us (4%)
  starting transfers between devices  16.6 us (2%)
  between operations  14.3 us (2%)
  matrix products  9.65 us (1%)
    psum x1, waiting for transfers between devices, local(): lax.psum((top_local, bottom_local, hot_local), ('rep', 'row'))  469 us
    psum x1, waiting for transfers between devices, local(): lax.psum(owner_grad.astype(jnp.bfloat16), 'rep').astype(jnp.float32)  123 us
    scatter-add x1, other arithmetic, local(): jax.ops.segment_sum(cold_terms, cold_bags.reshape(-1), num_segments=row_c...  44.7 us
    all_to_all x1, blocking collectives, local(): lax.all_to_all(asked, 'row', split_axis=0, concat_axis=0, tiled=True)  30 us
    gather x1, local copies, waits for them, and re-layouts, local(): cold_pool = jnp.sum(fetched[cold_bags].astype(jnp.float32), axis=1)  29.5 us
    scatter-add x1, other arithmetic, local(): jax.ops.segment_sum(hot_terms, hot_bags.reshape(-1), num_segments=hot_rows)  23 us
    scatter-add x1, other arithmetic, local(): jax.ops.segment_sum(arrived.reshape(-1, width).astype(jnp.float32), shard...  17.8 us
  transfers between devices with their start and end apart: 4, of which 3 were waited for; matrix products, arithmetic and copies ran while one was open for 8% of the time, Pallas kernels for 0%

commit v1 on v0

v1 whole, which is shorter than its diff:
```python
import jax
import jax.numpy as jnp
from jax import lax
from jax.experimental import pallas as pl
from jax.experimental.pallas import tpu as pltpu
from jax.sharding import PartitionSpec as P

E = 128
D_BOT = 256
H_TOP = 1024
B_DEV = 512
L = 16
LH = 8
CAP = 64
ROWS_DEV = 4096
HOT = 512
N_ROW = 48
N_REP = 16
SLOTS = N_ROW * CAP
NX, NY, NZ, NC = 4, 8, 12, 2

W_BOTTOM = 3 * E * (H_TOP // E)
W_HOT = W_BOTTOM + D_BOT
W_USED = W_HOT + HOT
W_ROWS = 4096
W_C = W_ROWS // NC
W_X = W_C // NX
W_Y = W_X // NY
W_Z = 8

G_C = ROWS_DEV // NC
G_Y = G_C // NY

BF = jnp.bfloat16
F32 = jnp.float32
VMEM_LIMIT = 56 * 1024 * 1024


def vmem():
    return pl.BlockSpec(memory_space=pltpu.VMEM)


def remote(src, dst, send_sem, recv_sem, device):
    return pltpu.make_async_remote_copy(
        src_ref=src,
        dst_ref=dst,
        send_sem=send_sem,
        recv_sem=recv_sem,
        device_id=device,
        device_id_type=pl.DeviceIdType.MESH,
    )


def signal(sem, device):
    pl.semaphore_signal(sem, inc=1, device_id=device, device_id_type=pl.DeviceIdType.MESH)


def position():
    rep = lax.axis_index("rep")
    row = lax.axis_index("row")
    return rep, row


def silu_slope(value):
    sigma = jax.nn.sigmoid(value)
    return sigma * (1.0 + value * (1.0 - sigma))


def fetch_kernel(
    req_ref, table_ref, out_ref, ids_ref, ids_smem, table32, stage32, stage, req_send, req_recv,
    row_send, row_recv, local_sem,
):
    rep, me = position()
    barrier = pltpu.get_barrier_semaphore()

    def greet(k, carry):
        signal(barrier, (rep, lax.rem(me + k, N_ROW)))
        return carry

    lax.fori_loop(1, N_ROW, greet, 0)
    pl.semaphore_wait(barrier, N_ROW - 1)

    def req_copy(k):
        peer = lax.rem(me + k, N_ROW)
        return remote(
            req_ref.at[peer], ids_ref.at[me], req_send.at[k], req_recv.at[me], (rep, peer)
        )

    def ask(k, carry):
        req_copy(k).start()
        return carry

    lax.fori_loop(1, N_ROW, ask, 0)
    own = pltpu.make_async_copy(req_ref.at[me], ids_ref.at[me], local_sem)
    own.start()

    def widen(i, carry):
        rows = pl.ds(pl.multiple_of(i * 256, 256), 256)
        table32[rows, :] = table_ref[rows, :].astype(F32)
        return carry

    lax.fori_loop(0, ROWS_DEV // 256, widen, 0)
    own.wait()

    def asked(k, carry):
        peer = lax.rem(me + k, N_ROW)
        remote(
            req_ref.at[peer], ids_ref.at[peer], req_send.at[k], req_recv.at[peer], (rep, peer)
        ).wait_recv()
        req_copy(k).wait_send()
        return carry

    lax.fori_loop(1, N_ROW, asked, 0)
    read = pltpu.make_async_copy(ids_ref, ids_smem, local_sem)
    read.start()
    read.wait()

    def row_copy(k):
        peer = lax.rem(me + k, N_ROW)
        return remote(
            stage.at[peer], out_ref.at[me], row_send.at[k], row_recv.at[me], (rep, peer)
        )

    def pick(peer):
        for i in range(CAP):
            row = ids_smem[peer, 0, i]
            stage32[pl.ds(i, 1), :] = table32[pl.ds(row, 1), :]
        return stage32[...].astype(BF)

    def serve(k, carry):
        peer = lax.rem(me + k, N_ROW)
        stage[peer] = pick(peer)
        row_copy(k).start()
        return carry

    lax.fori_loop(1, N_ROW, serve, 0)
    out_ref[me] = pick(me)

    def served(k, carry):
        peer = lax.rem(me + k, N_ROW)
        remote(
            stage.at[peer], out_ref.at[peer], row_send.at[k], row_recv.at[peer], (rep, peer)
        ).wait_recv()
        row_copy(k).wait_send()
        return carry

    lax.fori_loop(1, N_ROW, served, 0)


def fetch(requests, table):
    return pl.pallas_call(
        fetch_kernel,
        out_shape=(
            jax.ShapeDtypeStruct((N_ROW, CAP, E), BF),
            jax.ShapeDtypeStruct((N_ROW, 1, 128), jnp.int32),
        ),
        in_specs=[vmem(), vmem()],
        out_specs=(vmem(), vmem()),
        scratch_shapes=[
            pltpu.SMEM((N_ROW, 1, 128), jnp.int32),
            pltpu.VMEM((ROWS_DEV, E), F32),
            pltpu.VMEM((CAP, E), F32),
            pltpu.VMEM((N_ROW, CAP, E), BF),
            pltpu.SemaphoreType.DMA((N_ROW,)),
            pltpu.SemaphoreType.DMA((N_ROW,)),
            pltpu.SemaphoreType.DMA((N_ROW,)),
            pltpu.SemaphoreType.DMA((N_ROW,)),
            pltpu.SemaphoreType.DMA,
        ],
        compiler_params=pltpu.CompilerParams(
            collective_id=0, has_side_effects=True, vmem_limit_bytes=VMEM_LIMIT
        ),
        name="fetch",
    )(requests, table)


def contract_first(a, b):
    return lax.dot_general(a, b, (((0,), (0,)), ((), ())), preferred_element_type=F32)


def contract_last(a, b):
    return lax.dot_general(a, b, (((1,), (1,)), ((), ())), preferred_element_type=F32)


def mlp_kernel(
    fetched_ref, cold_ref, hot_ref, dense_ref, up_ref, bw_ref, tw_ref, table_ref, slot_ref, w_ref,
    cold_counts, hot_counts, feats, feats_t, fgrad,
):
    low = lax.broadcasted_iota(jnp.int32, (128, 128), 0)

    def count(j, carry):
        lanes = pl.ds(pl.multiple_of(j * 128, 128), 128)
        ids = cold_ref[:, lanes]
        lo = ids & 127
        hi = ids >> 7
        word = (hi * 43) >> 8
        amount = jnp.left_shift(jnp.ones_like(hi), 5 * (hi - 6 * word))
        for w in range(4):
            key = jnp.where(word == w, lo, -1)
            total = jnp.zeros((128, 128), jnp.int32)
            for l in range(L):
                total += jnp.where(low == key[l : l + 1, :], amount[l : l + 1, :], 0)
            for f in range(6):
                slab = ((total >> (5 * f)) & 31).astype(F32).astype(BF)
                cold_counts[(6 * w + f) * 128 : (6 * w + f + 1) * 128, lanes] = slab
        ids = hot_ref[:, lanes]
        lo = ids & 127
        amount = jnp.left_shift(jnp.ones_like(ids), 4 * (ids >> 7))
        total = jnp.zeros((128, 128), jnp.int32)
        for l in range(LH):
            total += jnp.where(low == lo[l : l + 1, :], amount[l : l + 1, :], 0)
        for f in range(4):
            slab = ((total >> (4 * f)) & 15).astype(F32).astype(BF)
            hot_counts[f * 128 : (f + 1) * 128, lanes] = slab
        return carry

    lax.fori_loop(0, B_DEV // 128, count, 0)

    bottom_pre = jnp.dot(dense_ref[...], bw_ref[...], preferred_element_type=F32)
    lower = bottom_pre * jax.nn.sigmoid(bottom_pre)
    feats[:, 0:E] = lower.astype(BF)
    slope = silu_slope(bottom_pre)

    pool = contract_first(fetched_ref[...], cold_counts[...])
    feats[:, E : 2 * E] = pool.T.astype(BF)
    pool = contract_first(table_ref[...], hot_counts[...])
    feats[:, 2 * E : 3 * E] = pool.T.astype(BF)
    feats_t[...] = feats[...].astype(F32).T.astype(BF)

    fgrad[...] = jnp.zeros_like(fgrad)
    for h in range(H_TOP // 256):
        cols = slice(h * 256, (h + 1) * 256)
        weight = tw_ref[:, cols]
        pre = jnp.dot(feats[...], weight, preferred_element_type=F32)
        delta = (up_ref[:, cols].astype(F32) * silu_slope(pre)).astype(BF)
        top = jnp.dot(feats_t[...], delta, preferred_element_type=F32).astype(BF)
        w_ref[768 * h : 768 * h + 384, :] = top[:, 0:128]
        w_ref[768 * h + 384 : 768 * h + 768, :] = top[:, 128:256]
        fgrad[...] += contract_last(delta, weight)

    bottom_delta = (fgrad[:, 0:E] * slope).astype(BF)
    w_ref[W_BOTTOM:W_HOT, :] = contract_first(dense_ref[...], bottom_delta).astype(BF)
    hot_back = fgrad[:, 2 * E : 3 * E].astype(BF)
    w_ref[W_HOT:W_USED, :] = jnp.dot(
        hot_counts[...], hot_back, preferred_element_type=F32
    ).astype(BF)
    w_ref[W_USED:W_ROWS, :] = jnp.zeros((W_ROWS - W_USED, E), BF)
    cold_back = fgrad[:, E : 2 * E].astype(BF)
    for s in range(SLOTS // 512):
        rows = slice(s * 512, (s + 1) * 512)
        slot_ref[rows, :] = jnp.dot(
            cold_counts[rows, :], cold_back, preferred_element_type=F32
        ).astype(BF)


def mlp(fetched, cold_bags, hot_bags, dense, upstream, bottom_weight, top_weight, hot_table):
    return pl.pallas_call(
        mlp_kernel,
        out_shape=(
            jax.ShapeDtypeStruct((SLOTS, E), BF),
            jax.ShapeDtypeStruct((W_ROWS, E), BF),
        ),
        in_specs=[vmem()] * 8,
        out_specs=(vmem(), vmem()),
        scratch_shapes=[
            pltpu.VMEM((SLOTS, B_DEV), BF),
            pltpu.VMEM((HOT, B_DEV), BF),
            pltpu.VMEM((B_DEV, 3 * E), BF),
            pltpu.VMEM((3 * E, B_DEV), BF),
            pltpu.VMEM((B_DEV, 3 * E), F32),
        ],
        compiler_params=pltpu.CompilerParams(vmem_limit_bytes=VMEM_LIMIT),
        name="mlp",
    )(fetched, cold_bags, hot_bags, dense, upstream, bottom_weight, top_weight, hot_table)


def back_kernel(
    slot_ref, w_ref, out_ref, sum_ref, part_c, half, part_x, quarter, part_y, eighth, part_z,
    row_send, row_recv, c_sem, x_send, x_recv, y_send, y_recv, z_send, z_recv, local_sem,
):
    rep, me = position()
    y, core = rep // NC, lax.rem(rep, NC)
    x, z = me // NZ, lax.rem(me, NZ)
    sibling = (y * NC + 1 - core, me)
    barrier = pltpu.get_barrier_semaphore()

    def greet(k, carry):
        signal(barrier, (rep, lax.rem(me + k, N_ROW)))
        return carry

    signal(barrier, sibling)

    def greet_y(k, carry):
        signal(barrier, (lax.rem(y + k, NY) * NC + core, me))
        return carry

    lax.fori_loop(1, NY, greet_y, 0)
    lax.fori_loop(1, N_ROW, greet, 0)
    pl.semaphore_wait(barrier, N_ROW - 1 + NY - 1 + 1)

    def half_rows(c):
        return pl.ds(pl.multiple_of(c * W_C, W_C), W_C)

    to_core = remote(
        w_ref.at[half_rows(1 - core)], part_c, c_sem.at[0], c_sem.at[1], sibling
    )
    to_core.start()

    def row_copy(k):
        peer = lax.rem(me + k, N_ROW)
        return remote(
            slot_ref.at[peer], out_ref.at[me], row_send.at[k], row_recv.at[me], (rep, peer)
        )

    def send(k, carry):
        row_copy(k).start()
        return carry

    lax.fori_loop(1, N_ROW, send, 0)
    own = pltpu.make_async_copy(slot_ref.at[me], out_ref.at[me], local_sem)
    own.start()

    to_core.wait()

    def add_c(i, carry):
        rows = pl.ds(pl.multiple_of(i * 256, 256), 256)
        mine = pl.ds(pl.multiple_of(core * W_C + i * 256, 256), 256)
        half[rows, :] = (w_ref[mine, :].astype(F32) + part_c[rows, :].astype(F32)).astype(BF)
        return carry

    lax.fori_loop(0, W_C // 256, add_c, 0)

    copies = []
    for k in range(1, NX):
        px = lax.rem(x + k, NX)
        copies.append(
            remote(
                half.at[pl.ds(pl.multiple_of(px * W_X, W_X), W_X)], part_x.at[k - 1],
                x_send.at[k - 1], x_recv.at[k - 1], (rep, px * NZ + z),
            )
        )
        copies[-1].start()
    for copy in copies:
        copy.wait()
    total = half[pl.ds(pl.multiple_of(x * W_X, W_X), W_X), :].astype(F32)
    for k in range(1, NX):
        total += part_x[k - 1].astype(F32)
    quarter[...] = total.astype(BF)

    copies = []
    for k in range(1, NY):
        py = lax.rem(y + k, NY)
        copies.append(
            remote(
                quarter.at[pl.ds(pl.multiple_of(py * W_Y, W_Y), W_Y)], part_y.at[k - 1],
                y_send.at[k - 1], y_recv.at[k - 1], (py * NC + core, me),
            )
        )
        copies[-1].start()
    for copy in copies:
        copy.wait()
    total = quarter[pl.ds(pl.multiple_of(y * W_Y, W_Y), W_Y), :].astype(F32)
    for k in range(1, NY):
        total += part_y[k - 1].astype(F32)
    eighth[0:W_Y, :] = total
    eighth[W_Y : NZ * W_Z, :] = jnp.zeros((NZ * W_Z - W_Y, E), F32)

    copies = []
    for k in range(1, NZ):
        pz = lax.rem(z + k, NZ)
        copies.append(
            remote(
                eighth.at[pl.ds(pl.multiple_of(pz * W_Z, W_Z), W_Z)], part_z.at[k - 1],
                z_send.at[k - 1], z_recv.at[k - 1], (rep, x * NZ + pz),
            )
        )
        copies[-1].start()
    for copy in copies:
        copy.wait()
    total = eighth[pl.ds(pl.multiple_of(z * W_Z, W_Z), W_Z), :]
    for k in range(1, NZ):
        total += part_z[k - 1]
    sum_ref[...] = total

    own.wait()

    def sent(k, carry):
        peer = lax.rem(me + k, N_ROW)
        remote(
            slot_ref.at[peer], out_ref.at[peer], row_send.at[k], row_recv.at[peer], (rep, peer)
        ).wait_recv()
        row_copy(k).wait_send()
        return carry

    lax.fori_loop(1, N_ROW, sent, 0)


def back(slot_grad, w):
    dma = pltpu.SemaphoreType.DMA
    return pl.pallas_call(
        back_kernel,
        out_shape=(
            jax.ShapeDtypeStruct((N_ROW, CAP, E), BF),
            jax.ShapeDtypeStruct((W_Z, E), F32),
        ),
        in_specs=[vmem(), vmem()],
        out_specs=(vmem(), vmem()),
        scratch_shapes=[
            pltpu.VMEM((W_C, E), BF),
            pltpu.VMEM((W_C, E), BF),
            pltpu.VMEM((NX - 1, W_X, E), BF),
            pltpu.VMEM((W_X, E), BF),
            pltpu.VMEM((NY - 1, W_Y, E), BF),
            pltpu.VMEM((NZ * W_Z, E), F32),
            pltpu.VMEM((NZ - 1, W_Z, E), F32),
            dma((N_ROW,)),
            dma((N_ROW,)),
            dma((2,)),
            dma((NX - 1,)),
            dma((NX - 1,)),
            dma((NY - 1,)),
            dma((NY - 1,)),
            dma((NZ - 1,)),
            dma((NZ - 1,)),
            dma,
        ],
        compiler_params=pltpu.CompilerParams(
            collective_id=1, has_side_effects=True, vmem_limit_bytes=VMEM_LIMIT
        ),
        name="back",
    )(slot_grad, w)


def owner_kernel(ids_ref, arrived_ref, out_ref):
    def block(i, carry):
        rows = pl.multiple_of(i * 256, 256)
        index = lax.broadcasted_iota(jnp.int32, (256, SLOTS), 0) + rows
        hits = jnp.where(index == ids_ref[...], 1.0, 0.0).astype(BF)
        total = jnp.dot(hits, arrived_ref[...], preferred_element_type=F32)
        out_ref[pl.ds(rows, 256), :] = total.astype(BF)
        return carry

    lax.fori_loop(0, ROWS_DEV // 256, block, 0)


def owner(ids, arrived):
    return pl.pallas_call(
        owner_kernel,
        out_shape=jax.ShapeDtypeStruct((ROWS_DEV, E), BF),
        in_specs=[vmem(), vmem()],
        out_specs=vmem(),
        compiler_params=pltpu.CompilerParams(vmem_limit_bytes=VMEM_LIMIT),
        name="owner",
    )(ids, arrived)


def share_kernel(
    cold_ref, sum_ref, cold_out, w_out, got_c, mine, got_y, final, gath_z, w_y, gath_y, gath_x,
    c_send, c_recv, y_send, y_recv, a_send, a_recv, b_send, b_recv,
    wz_send, wz_recv, wy_send, wy_recv, wx_send, wx_recv, wc_sem,
):
    rep, me = position()
    y, core = rep // NC, lax.rem(rep, NC)
    x, z = me // NZ, lax.rem(me, NZ)
    sibling = (y * NC + 1 - core, me)
    barrier = pltpu.get_barrier_semaphore()

    def y_peer(k):
        return (lax.rem(y + k, NY) * NC + core, me)

    def x_peer(k):
        return (rep, lax.rem(x + k, NX) * NZ + z)

    def z_peer(k):
        return (rep, x * NZ + lax.rem(z + k, NZ))

    signal(barrier, sibling)
    for k in range(1, NY):
        signal(barrier, y_peer(k))
    for k in range(1, NX):
        signal(barrier, x_peer(k))
    for k in range(1, NZ):
        signal(barrier, z_peer(k))
    pl.semaphore_wait(barrier, 1 + NY - 1 + NX - 1 + NZ - 1)

    def g_rows(c, j):
        return pl.ds(pl.multiple_of(c * G_C + j * G_Y, G_Y), G_Y)

    to_core = []
    for k in range(1, NY + 1):
        j = lax.rem(y + k, NY)
        to_core.append(
            remote(
                cold_ref.at[g_rows(1 - core, j)], got_c.at[k - 1], c_send.at[k - 1],
                c_recv.at[k - 1], sibling,
            )
        )
        to_core[-1].start()
    gath_z[0] = sum_ref[...]
    over_z = []
    for k in range(1, NZ):
        over_z.append(
            remote(sum_ref, gath_z.at[k], wz_send.at[k - 1], wz_recv.at[k - 1], z_peer(k))
        )
        over_z[-1].start()

    over_y = []
    for k in range(1, NY + 1):
        j = lax.rem(y + k, NY)
        to_core[k - 1].wait_recv()
        total = cold_ref[g_rows(core, j), :].astype(F32) + got_c[k - 1].astype(F32)
        if k < NY:
            mine[k - 1] = total.astype(BF)
            over_y.append(
                remote(
                    mine.at[k - 1], got_y.at[k - 1], y_send.at[k - 1], y_recv.at[k - 1], y_peer(k)
                )
            )
            over_y[-1].start()

    for copy in over_z:
        copy.wait()

    def place(k, carry):
        owner_z = lax.rem(z - k + NZ, NZ)
        w_y[pl.ds(pl.multiple_of(owner_z * W_Z, W_Z), W_Z), :] = gath_z[k]
        return carry

    lax.fori_loop(0, NZ, place, 0)
    gath_y[y] = w_y[0:W_Y, :].astype(BF)
    w_over_y = []
    for k in range(1, NY):
        w_over_y.append(
            remote(gath_y.at[y], gath_y.at[y], wy_send.at[k - 1], wy_recv.at[k - 1], y_peer(k))
        )
        w_over_y[-1].start()

    for k in range(1, NY):
        over_y[k - 1].wait_recv()
        total += got_y[k - 1].astype(F32)
    final[...] = total.astype(BF)
    share_y = []
    for k in range(1, NY):
        share_y.append(
            remote(
                final, cold_out.at[g_rows(core, y)], a_send.at[k - 1], a_recv.at[k - 1], y_peer(k)
            )
        )
        share_y[-1].start()
    share_c = [
        remote(final, cold_out.at[g_rows(core, y)], b_send.at[0], b_recv.at[0], sibling)
    ]
    share_c[0].start()
    cold_out[g_rows(core, y), :] = final[...]

    for copy in w_over_y:
        copy.wait()
    w_over_x = []
    for k in range(1, NX):
        w_over_x.append(
            remote(gath_y, gath_x.at[x], wx_send.at[k - 1], wx_recv.at[k - 1], x_peer(k))
        )
        w_over_x[-1].start()
    gath_x[x] = gath_y[...]

    for k in range(1, NY):
        share_y[k - 1].wait_recv()
        j = lax.rem(y - k + NY, NY)
        rows = cold_out.at[g_rows(core, j)]
        share_c.append(remote(rows, rows, b_send.at[k], b_recv.at[k], sibling))
        share_c[-1].start()

    for copy in w_over_x:
        copy.wait()
    w_over_c = remote(gath_x, w_out.at[core], wc_sem.at[0], wc_sem.at[1], sibling)
    w_over_c.start()
    w_out[core] = gath_x[...]

    for copy in to_core + over_y + share_y:
        copy.wait_send()
    for copy in share_c:
        copy.wait()
    w_over_c.wait()


def share(cold, part):
    dma = pltpu.SemaphoreType.DMA
    return pl.pallas_call(
        share_kernel,
        out_shape=(
            jax.ShapeDtypeStruct((ROWS_DEV, E), BF),
            jax.ShapeDtypeStruct((NC, NX, NY, W_Y, E), BF),
        ),
        in_specs=[vmem(), vmem()],
        out_specs=(vmem(), vmem()),
        scratch_shapes=[
            pltpu.VMEM((NY, G_Y, E), BF),
            pltpu.VMEM((NY - 1, G_Y, E), BF),
            pltpu.VMEM((NY - 1, G_Y, E), BF),
            pltpu.VMEM((G_Y, E), BF),
            pltpu.VMEM((NZ, W_Z, E), F32),
            pltpu.VMEM((NZ * W_Z, E), F32),
            pltpu.VMEM((NY, W_Y, E), BF),
            pltpu.VMEM((NX, NY, W_Y, E), BF),
            dma((NY,)),
            dma((NY,)),
            dma((NY - 1,)),
            dma((NY - 1,)),
            dma((NY - 1,)),
            dma((NY - 1,)),
            dma((NY,)),
            dma((NY,)),
            dma((NZ - 1,)),
            dma((NZ - 1,)),
            dma((NY - 1,)),
            dma((NY - 1,)),
            dma((NX - 1,)),
            dma((NX - 1,)),
            dma((2,)),
        ],
        compiler_params=pltpu.CompilerParams(
            collective_id=2, has_side_effects=True, vmem_limit_bytes=VMEM_LIMIT
        ),
        name="share",
    )(cold, part)


def local(
    dense_act,
    upstream,
    bottom_weight,
    top_weight,
    hot_table,
    cold_table,
    hot_bags,
    cold_bags,
    requests,
):
    asked = jnp.pad(requests.reshape(N_ROW, 1, CAP), ((0, 0), (0, 0), (0, 128 - CAP)))
    fetched, ids = fetch(asked, cold_table)
    slot_grad, w = mlp(
        fetched.reshape(SLOTS, E), cold_bags.T, hot_bags.T, dense_act, upstream, bottom_weight,
        top_weight, hot_table,
    )
    arrived, part = back(slot_grad.reshape(N_ROW, CAP, E), w)
    owned = owner(ids[:, 0, :CAP].reshape(1, SLOTS), arrived.reshape(SLOTS, E))
    cold, summed = share(owned, part)
    cold_grad = cold.astype(F32)
    summed = summed.reshape(W_ROWS, E)
    top_grad = (
        summed[:W_BOTTOM]
        .reshape(H_TOP // E, 3 * E, E)
        .transpose(1, 0, 2)
        .reshape(3 * E, H_TOP)
        .astype(F32)
    )
    bottom_grad = summed[W_BOTTOM:W_HOT].astype(F32)
    hot_grad = summed[W_HOT:W_USED].astype(F32)
    return (top_grad, bottom_grad, hot_grad, cold_grad)


def solution(mesh):
    placed = (
        P(("rep", "row"), None),
        P(("rep", "row"), None),
        P(),
        P(),
        P(),
        P("row", None),
        P(("rep", "row"), None),
        P(("rep", "row"), None),
        P("rep", "row", None, None),
    )
    return jax.shard_map(
        local,
        mesh=mesh,
        in_specs=placed,
        out_specs=(P(), P(), P(), P("row", None)),
        check_vma=False,
    )
```

time: 835 us -> 178 us (0.21)
  waiting for transfers between devices: 605 us -> 0 us
  Pallas kernels: 0 us -> 166 us
  other arithmetic: 94.4 us -> 5.92 us
  local copies, waits for them, and re-layouts: 65.1 us -> 4.15 us
  blocking collectives: 30 us -> 0 us
  starting transfers between devices: 16.6 us -> 0 us
  between operations: 14.3 us -> 0.67 us
  matrix products: 9.65 us -> 0 us
    psum x2 -> x0, waiting for transfers between devices: 592 us -> none  [the longest x1 469 us: local(): lax.psum((top_local, bottom_local, hot_local), ('rep', 'row'))]
    pallas_call x0 -> x5, Pallas kernels: none -> 166 us  [the longest x1 56.4 us: fetch(): pl.pallas_call(fetch_kernel, out_shape=(jax.ShapeDtypeStruct((N_ROW, CAP,...]
    scatter-add x3 -> x0, other arithmetic: 85.5 us -> none  [the longest x1 44.7 us: local(): jax.ops.segment_sum(cold_terms, cold_bags.reshape(-1), num_segments=row_c...]
    gather x3 -> x0, local copies, waits for them, and re-layouts: 53.2 us -> none  [the longest x1 29.5 us: local(): cold_pool = jnp.sum(fetched[cold_bags].astype(jnp.float32), axis=1)]
    all_to_all x1 -> x0, blocking collectives: 30 us -> none  [local(): lax.all_to_all(asked, 'row', split_axis=0, concat_axis=0, tiled=True)]
    all_to_all x2 -> x0, starting transfers between devices: 16.3 us -> none  [the longest x1 11.6 us: local(): lax.all_to_all(slot_grad, 'row', split_axis=0, concat_axis=0, tiled=True)]
    all_to_all x2 -> x0, waiting for transfers between devices: 12.8 us -> none  [the longest x1 12.8 us: local(): lax.all_to_all(gathered, 'row', split_axis=0, concat_axis=0, tiled=True)]
    dot_general x5 -> x0, matrix products: 9.65 us -> none  [the longest x1 2.63 us: local(): jnp.dot(features.T, top_delta, preferred_element_type=jnp.float32)]
  transfers between devices with their start and end apart: 4 -> 0, of which waited for: 3 -> 0; matrix products, arithmetic and copies ran while one was open for 8% -> 0% of each run, Pallas kernels for 0% -> 0%
where the time goes in v1:
time: 178 us; the launch traced here: 177 us
  Pallas kernels  166 us (93%)
  other arithmetic  5.92 us (3%)
  local copies, waits for them, and re-layouts  4.15 us (2%)
    pallas_call x1, Pallas kernels, fetch(): pl.pallas_call(fetch_kernel, out_shape=(jax.ShapeDtypeStruct((N_ROW, CAP,...  56.4 us
    pallas_call x1, Pallas kernels, share(): pl.pallas_call(share_kernel, out_shape=(jax.ShapeDtypeStruct((ROWS_DEV, E...  45.8 us
    pallas_call x1, Pallas kernels, back(): pl.pallas_call(back_kernel, out_shape=(jax.ShapeDtypeStruct((N_ROW, CAP,...  42 us
    pallas_call x1, Pallas kernels, owner(): pl.pallas_call(owner_kernel, out_shape=jax.ShapeDtypeStruct((ROWS_DEV, E)...  11.1 us
    pallas_call x1, Pallas kernels, mlp(): pl.pallas_call(mlp_kernel, out_shape=(jax.ShapeDtypeStruct((SLOTS, E), BF...  10.9 us

profile of v1, /device:TPU:1, one launch (start us, length us, event | category | flops | bytes accessed | tf_op | source)
XLA Modules:
  0.0 177.0 jit_solution(4820880796191536316)
XLA Ops:
  0.6 1.4 pad.4.req_ref
  2.0 56.4 %fetch.1 = (bf16[48,64,128]{2,1,0:T(8,128)(2,1)}, s32[48,1,128]{2,1,0:T(1,128)}) custom-call(s32[48,1,128]{2,1,0:T(1,128)} %pad.4.req_ref, bf16[4096,128]{1,0:T(8,128)(2,1)} %table_ref.2), custom_call_target="tpu_custom_call" | custom-call | tf_op jit(solution)/shard_map/fetch/pallas_call | solution.py:151
  58.4 0.8 slice_reduce_fusion
  59.2 0.7 reshape_squeeze.3.ids_ref
  59.9 10.9 %mlp.1 = (bf16[3072,128]{1,0:T(8,128)(2,1)}, bf16[4096,128]{1,0:T(8,128)(2,1)}) custom-call(bf16[3072,128]{1,0:T(8,128)(2,1)} %bitcast.21, s32[16,512]{1,0:T(8,128)} %bitcast.22, s32[8,512]{1,0:T(8,128)} %bitcast.24, bf16[512,256]{1,0:T(8,128)(2,1)} %dense_ref.1, bf16[512,1024]{1,0:T(8,128)(2,1)} %up_ref.1, bf16[256,128]{1,0:T(8,128)(2,1)} %bw_ref.1, ...), custom_call_target="tpu_custom_call" | custom-call | tf_op jit(solution)/shard_map/mlp/pallas_call | solution.py:257
  70.8 42.0 %back.1 = (bf16[48,64,128]{2,1,0:T(8,128)(2,1)}, f32[8,128]{1,0:T(8,128)}) custom-call(bf16[48,64,128]{2,1,0:T(8,128)(2,1)} %bitcast.19, bf16[4096,128]{1,0:T(8,128)(2,1)} %get-tuple-element.15.w_ref), custom_call_target="tpu_custom_call" | custom-call | tf_op jit(solution)/shard_map/back/pallas_call | solution.py:400
  112.8 11.1 %owner.1.cold_ref = bf16[4096,128]{1,0:T(8,128)(2,1)} custom-call(s32[1,3072]{1,0:T(1,128)} %reshape_squeeze.3.ids_ref, bf16[3072,128]{1,0:T(8,128)(2,1)} %bitcast.20), custom_call_target="tpu_custom_call" | custom-call | tf_op jit(solution)/shard_map/owner/pallas_call | solution.py:447
  124.0 45.8 %share.1 = (bf16[4096,128]{1,0:T(8,128)(2,1)}, bf16[2,4,8,64,128]{4,3,2,1,0:T(8,128)(2,1)}) custom-call(bf16[4096,128]{1,0:T(8,128)(2,1)} %owner.1.cold_ref, f32[8,128]{1,0:T(8,128)} %get-tuple-element.17.sum_ref), custom_call_target="tpu_custom_call" | custom-call | tf_op jit(solution)/shard_map/share/pallas_call | solution.py:588
  169.7 1.5 slice_convert_fusion.1
  171.2 1.6 slice_convert_fusion
  172.9 1.2 slice.16
  174.1 0.0 copy-start
  174.1 1.3 copy_bitcast_fusion
  175.4 0.1 copy-done
  175.5 1.5 convert_element_type.27
Async XLA Ops:
  174.1 1.5 copy-start

commit v2 on v0

v2 whole, which is shorter than its diff:
```python
import jax
import jax.numpy as jnp
from jax import lax
from jax.experimental import pallas as pl
from jax.experimental.pallas import tpu as pltpu
from jax.sharding import PartitionSpec as P

E = 128
D_BOT = 256
H_TOP = 1024
B_DEV = 512
L = 16
LH = 8
CAP = 64
ROWS_DEV = 4096
HOT = 512
N_ROW = 48
N_REP = 16
SLOTS = N_ROW * CAP
NX, NY, NZ, NC = 4, 8, 12, 2

W_BOTTOM = 3 * E * (H_TOP // E)
W_HOT = W_BOTTOM + D_BOT
W_USED = W_HOT + HOT
W_ROWS = 4096
W_C = W_ROWS // NC
W_X = W_C // NX
W_Y = W_X // NY
W_Z = 8

G_C = ROWS_DEV // NC
G_Y = G_C // NY

BF = jnp.bfloat16
F32 = jnp.float32
VMEM_LIMIT = 56 * 1024 * 1024


def vmem():
    return pl.BlockSpec(memory_space=pltpu.VMEM)


def remote(src, dst, send_sem, recv_sem, device):
    return pltpu.make_async_remote_copy(
        src_ref=src,
        dst_ref=dst,
        send_sem=send_sem,
        recv_sem=recv_sem,
        device_id=device,
        device_id_type=pl.DeviceIdType.MESH,
    )


def signal(sem, device):
    pl.semaphore_signal(sem, inc=1, device_id=device, device_id_type=pl.DeviceIdType.MESH)


def position():
    rep = lax.axis_index("rep")
    row = lax.axis_index("row")
    return rep, row


def silu_slope(value):
    sigma = jax.nn.sigmoid(value)
    return sigma * (1.0 + value * (1.0 - sigma))


def contract_first(a, b):
    return lax.dot_general(a, b, (((0,), (0,)), ((), ())), preferred_element_type=F32)


def contract_last(a, b):
    return lax.dot_general(a, b, (((1,), (1,)), ((), ())), preferred_element_type=F32)


def offset(k, core):
    dx = k % NX
    j = k // NX
    dz = (j + 1) // 2 if j % 2 else -(j // 2)
    return dx, dz * (1 - 2 * core)


def offset_of(k, core):
    dx = lax.rem(k, NX)
    j = lax.div(k, NX)
    odd = lax.rem(j, 2)
    dz = odd * lax.div(j + 1, 2) - (1 - odd) * lax.div(j, 2)
    return dx, dz * (1 - 2 * core)


def step_kernel(
    req_ref, cold_ref, hot_ref, bw_ref, table_any, dense_any, up_any, tw_any, hott_any,
    cold_out, w_out, rows_any, arr_any,
    req_pad, ids_v, ids_smem, table, table32, stage32, stage, fetched,
    dense_ref, up_ref, tw_ref, hott_ref, cold_counts, hot_counts, feats, feats_t, deltas, fgrad,
    slot, w_ref, arr_v, acc, cold_b,
    part_c, half, part_x, quarter, part_y, eighth, part_z, summed,
    got_c, mine, got_y, final, gath_z, w_y, gath_y, gath_x,
    load_sem, req_send, req_recv, row_send, row_recv, arr_send, arr_recv, arr_sem,
    wc, rx_send, rx_recv, ry_send, ry_recv, rz_send, rz_recv,
    c_send, c_recv, y_send, y_recv, a_send, a_recv, b_send, b_recv,
    wz_send, wz_recv, wy_send, wy_recv, wx_send, wx_recv, wc_sem,
):
    rep, me = position()
    y, core = rep // NC, lax.rem(rep, NC)
    x, z = me // NZ, lax.rem(me, NZ)
    sibling = (y * NC + 1 - core, me)

    def to(k):
        dx, dz = offset(k, core)
        return lax.rem(x + dx, NX) * NZ + lax.rem(z + dz + NZ, NZ)

    def y_peer(k):
        return (lax.rem(y + k, NY) * NC + core, me)

    def x_peer(k):
        return (rep, lax.rem(x + k, NX) * NZ + z)

    def z_peer(k):
        return (rep, x * NZ + lax.rem(z + k, NZ))

    loads = []
    for i, (src, dst) in enumerate(
        (
            (table_any, table), (dense_any, dense_ref), (up_any, up_ref), (tw_any, tw_ref),
            (hott_any, hott_ref),
        )
    ):
        loads.append(pltpu.make_async_copy(src, dst, load_sem.at[i]))
        loads[-1].start()

    barrier = pltpu.get_barrier_semaphore()
    for k in range(1, N_ROW):
        signal(barrier, (rep, to(k)))
    signal(barrier, sibling)
    for k in range(1, NY):
        signal(barrier, y_peer(k))
    req_pad[:, :, 0:CAP] = req_ref[...]
    req_pad[:, :, CAP:128] = jnp.zeros((N_ROW, 1, 128 - CAP), jnp.int32)
    pl.semaphore_wait(barrier, N_ROW - 1 + 1 + NY - 1)

    asks = [None]
    for k in range(1, N_ROW):
        peer = to(k)
        asks.append(
            remote(req_pad.at[peer], ids_v.at[k], req_send.at[k], req_recv.at[k], (rep, peer))
        )
        asks[-1].start()
    ids_v[0] = req_pad[me]

    loads[0].wait()

    def widen(i, carry):
        rows = pl.ds(pl.multiple_of(i * 256, 256), 256)
        table32[rows, :] = table[rows, :].astype(F32)
        return carry

    lax.fori_loop(0, ROWS_DEV // 256, widen, 0)

    low = lax.broadcasted_iota(jnp.int32, (128, 128), 0)

    def count(j, carry):
        lanes = pl.ds(pl.multiple_of(j * 128, 128), 128)
        ids = cold_ref[:, lanes]
        lo = ids & 127
        hi = ids >> 7
        word = (hi * 43) >> 8
        amount = jnp.left_shift(jnp.ones_like(hi), 5 * (hi - 6 * word))
        for w in range(4):
            key = jnp.where(word == w, lo, -1)
            total = jnp.zeros((128, 128), jnp.int32)
            for l in range(L):
                total += jnp.where(low == key[l : l + 1, :], amount[l : l + 1, :], 0)
            for f in range(6):
                slab = ((total >> (5 * f)) & 31).astype(F32).astype(BF)
                cold_counts[(6 * w + f) * 128 : (6 * w + f + 1) * 128, lanes] = slab
        ids = hot_ref[:, lanes]
        lo = ids & 127
        amount = jnp.left_shift(jnp.ones_like(ids), 4 * (ids >> 7))
        total = jnp.zeros((128, 128), jnp.int32)
        for l in range(LH):
            total += jnp.where(low == lo[l : l + 1, :], amount[l : l + 1, :], 0)
        for f in range(4):
            slab = ((total >> (4 * f)) & 15).astype(F32).astype(BF)
            hot_counts[f * 128 : (f + 1) * 128, lanes] = slab
        return carry

    lax.fori_loop(0, B_DEV // 256, count, 0)

    for k in range(1, N_ROW):
        asks[k].wait_recv()
    read = pltpu.make_async_copy(ids_v, ids_smem, load_sem.at[0])
    read.start()
    read.wait()

    def pick(k):
        for i in range(CAP):
            row = ids_smem[k, 0, i]
            stage32[pl.ds(i, 1), :] = table32[pl.ds(row, 1), :]
        stage[k] = stage32[...].astype(BF)

    def serve(k, carry):
        dx, dz = offset_of(k, core)
        peer = lax.rem(x - dx + NX, NX) * NZ + lax.rem(z - dz + NZ, NZ)
        pick(k)
        remote(
            stage.at[k], rows_any.at[me], row_send.at[k], row_recv.at[k], (rep, peer)
        ).start()
        return carry

    lax.fori_loop(1, N_ROW, serve, 0)
    pick(0)
    own = pltpu.make_async_copy(stage.at[0], rows_any.at[me], load_sem.at[0])
    own.start()

    lax.fori_loop(B_DEV // 256, B_DEV // 128, count, 0)
    loads[1].wait()
    bottom_pre = jnp.dot(dense_ref[...], bw_ref[...], preferred_element_type=F32)
    lower = bottom_pre * jax.nn.sigmoid(bottom_pre)
    feats[:, 0:E] = lower.astype(BF)
    slope = silu_slope(bottom_pre)
    fgrad[:, 0:E] = slope
    for i in range(2, 5):
        loads[i].wait()
    pool = contract_first(hott_ref[...], hot_counts[...])
    feats[:, 2 * E : 3 * E] = pool.T.astype(BF)

    own.wait()
    for k in range(1, N_ROW):
        owner_k = to(k)
        remote(
            stage.at[k], rows_any.at[owner_k], row_send.at[k], row_recv.at[k], (rep, owner_k)
        ).wait_recv()
    read = pltpu.make_async_copy(rows_any, fetched, load_sem.at[1])
    read.start()
    read.wait()

    pool = contract_first(fetched[...].reshape(SLOTS, E), cold_counts[...])
    feats[:, E : 2 * E] = pool.T.astype(BF)
    slope = fgrad[:, 0:E]
    for h in range(H_TOP // 256):
        cols = slice(h * 256, (h + 1) * 256)
        weight = tw_ref[:, cols]
        pre = jnp.dot(feats[...], weight, preferred_element_type=F32)
        delta = (up_ref[:, cols].astype(F32) * silu_slope(pre)).astype(BF)
        deltas[:, cols] = delta
        term = contract_last(delta, weight)
        if h == 0:
            fgrad[...] = term
        else:
            fgrad[...] += term
    cold_back = fgrad[:, E : 2 * E].astype(BF)
    for s in range(SLOTS // 512):
        total = jnp.dot(
            cold_counts[s * 512 : (s + 1) * 512, :], cold_back, preferred_element_type=F32
        )
        slot[8 * s : 8 * s + 8] = total.astype(BF).reshape(8, CAP, E)

    sends = [None]
    for k in range(1, N_ROW):
        peer = to(k)
        sends.append(
            remote(slot.at[peer], arr_any.at[k], arr_send.at[k], arr_recv.at[k], (rep, peer))
        )
        sends[-1].start()
    own = pltpu.make_async_copy(slot.at[me], arr_any.at[0], load_sem.at[0])
    own.start()

    feats_t[...] = feats[...].astype(F32).T.astype(BF)
    for h in range(H_TOP // 256):
        cols = slice(h * 256, (h + 1) * 256)
        top = jnp.dot(feats_t[...], deltas[:, cols], preferred_element_type=F32).astype(BF)
        w_ref[768 * h : 768 * h + 384, :] = top[:, 0:128]
        w_ref[768 * h + 384 : 768 * h + 768, :] = top[:, 128:256]
    bottom_delta = (fgrad[:, 0:E] * slope).astype(BF)
    w_ref[W_BOTTOM:W_HOT, :] = contract_first(dense_ref[...], bottom_delta).astype(BF)
    hot_back = fgrad[:, 2 * E : 3 * E].astype(BF)
    w_ref[W_HOT:W_USED, :] = jnp.dot(
        hot_counts[...], hot_back, preferred_element_type=F32
    ).astype(BF)
    w_ref[W_USED:W_ROWS, :] = jnp.zeros((W_ROWS - W_USED, E), BF)

    to_half = remote(
        w_ref.at[pl.ds(pl.multiple_of((1 - core) * W_C, W_C), W_C)], part_c, wc.at[0], wc.at[1],
        sibling,
    )
    to_half.start()

    lane = lax.broadcasted_iota(jnp.int32, (1, 128), 1)
    place512 = lax.broadcasted_iota(jnp.int32, (512, 256), 0)

    def arrive(g):
        for k in range(4 * g, 4 * g + 4):
            if k == 0:
                own.wait()
            else:
                sends[k].wait_recv()
        copy = pltpu.make_async_copy(arr_any.at[4 * g : 4 * g + 4], arr_v.at[g % 2], arr_sem.at[g % 2])
        copy.start()
        return copy

    def pair(k):
        return jnp.where(lane < CAP, ids_v[k], pltpu.roll(ids_v[k + 1], CAP, 1))

    def gather_in(g):
        wanted = jnp.concatenate([pair(4 * g), pair(4 * g + 2)], axis=1)
        values = arr_v[g % 2].reshape(4 * CAP, E)

        def block(i, carry):
            first = pl.multiple_of(i * 512, 512)
            hits = jnp.where(place512 == wanted - first, 1.0, 0.0).astype(BF)
            term = jnp.dot(hits, values, preferred_element_type=F32)
            rows = pl.ds(first, 512)
            if g == 0:
                acc[rows, :] = term
            elif g == N_ROW // 4 - 1:
                cold_b[rows, :] = (acc[rows, :] + term).astype(BF)
            else:
                acc[rows, :] += term
            return carry

        lax.fori_loop(0, ROWS_DEV // 512, block, 0)

    def groups(lo, hi, copy):
        for g in range(lo, hi):
            copy.wait()
            following = arrive(g + 1) if g + 1 < N_ROW // 4 else None
            gather_in(g)
            copy = following
        return copy

    copy = groups(0, 2, arrive(0))

    to_half.wait()

    def add_c(i, carry):
        rows = pl.ds(pl.multiple_of(i * 256, 256), 256)
        own_rows = pl.ds(pl.multiple_of(core * W_C + i * 256, 256), 256)
        half[rows, :] = (w_ref[own_rows, :].astype(F32) + part_c[rows, :].astype(F32)).astype(BF)
        return carry

    lax.fori_loop(0, W_C // 256, add_c, 0)
    to_x = []
    for k in range(1, NX):
        px = lax.rem(x + k, NX)
        to_x.append(
            remote(
                half.at[pl.ds(pl.multiple_of(px * W_X, W_X), W_X)], part_x.at[k - 1],
                rx_send.at[k - 1], rx_recv.at[k - 1], x_peer(k),
            )
        )
        to_x[-1].start()

    copy = groups(2, 6, copy)

    for c in to_x:
        c.wait()
    total = half[pl.ds(pl.multiple_of(x * W_X, W_X), W_X), :].astype(F32)
    for k in range(1, NX):
        total += part_x[k - 1].astype(F32)
    quarter[...] = total.astype(BF)
    to_y = []
    for k in range(1, NY):
        py = lax.rem(y + k, NY)
        to_y.append(
            remote(
                quarter.at[pl.ds(pl.multiple_of(py * W_Y, W_Y), W_Y)], part_y.at[k - 1],
                ry_send.at[k - 1], ry_recv.at[k - 1], y_peer(k),
            )
        )
        to_y[-1].start()

    copy = groups(6, 9, copy)

    for c in to_y:
        c.wait()
    total = quarter[pl.ds(pl.multiple_of(y * W_Y, W_Y), W_Y), :].astype(F32)
    for k in range(1, NY):
        total += part_y[k - 1].astype(F32)
    eighth[0:W_Y, :] = total
    eighth[W_Y : NZ * W_Z, :] = jnp.zeros((NZ * W_Z - W_Y, E), F32)
    to_z = []
    for k in range(1, NZ):
        pz = lax.rem(z + k, NZ)
        to_z.append(
            remote(
                eighth.at[pl.ds(pl.multiple_of(pz * W_Z, W_Z), W_Z)], part_z.at[k - 1],
                rz_send.at[k - 1], rz_recv.at[k - 1], z_peer(k),
            )
        )
        to_z[-1].start()

    groups(9, N_ROW // 4, copy)

    def g_rows(c, j):
        return pl.ds(pl.multiple_of(c * G_C + j * G_Y, G_Y), G_Y)

    to_core = []
    for k in range(1, NY + 1):
        j = lax.rem(y + k, NY)
        to_core.append(
            remote(
                cold_b.at[g_rows(1 - core, j)], got_c.at[k - 1], c_send.at[k - 1],
                c_recv.at[k - 1], sibling,
            )
        )
        to_core[-1].start()

    for c in to_z:
        c.wait()
    total = eighth[pl.ds(pl.multiple_of(z * W_Z, W_Z), W_Z), :]
    for k in range(1, NZ):
        total += part_z[k - 1]
    summed[...] = total
    gath_z[0] = total
    over_z = []
    for k in range(1, NZ):
        over_z.append(
            remote(summed, gath_z.at[k], wz_send.at[k - 1], wz_recv.at[k - 1], z_peer(k))
        )
        over_z[-1].start()

    over_y = []
    for k in range(1, NY + 1):
        j = lax.rem(y + k, NY)
        to_core[k - 1].wait_recv()
        total = cold_b[g_rows(core, j), :].astype(F32) + got_c[k - 1].astype(F32)
        if k < NY:
            mine[k - 1] = total.astype(BF)
            over_y.append(
                remote(
                    mine.at[k - 1], got_y.at[k - 1], y_send.at[k - 1], y_recv.at[k - 1], y_peer(k)
                )
            )
            over_y[-1].start()

    for c in over_z:
        c.wait()

    def place(k, carry):
        owner_z = lax.rem(z - k + NZ, NZ)
        w_y[pl.ds(pl.multiple_of(owner_z * W_Z, W_Z), W_Z), :] = gath_z[k]
        return carry

    lax.fori_loop(0, NZ, place, 0)
    gath_y[y] = w_y[0:W_Y, :].astype(BF)
    w_over_y = []
    for k in range(1, NY):
        w_over_y.append(
            remote(gath_y.at[y], gath_y.at[y], wy_send.at[k - 1], wy_recv.at[k - 1], y_peer(k))
        )
        w_over_y[-1].start()

    for k in range(1, NY):
        over_y[k - 1].wait_recv()
        total += got_y[k - 1].astype(F32)
    final[...] = total.astype(BF)
    share_y = []
    for k in range(1, NY):
        share_y.append(
            remote(
                final, cold_out.at[g_rows(core, y)], a_send.at[k - 1], a_recv.at[k - 1], y_peer(k)
            )
        )
        share_y[-1].start()
    share_c = [
        remote(final, cold_out.at[g_rows(core, y)], b_send.at[0], b_recv.at[0], sibling)
    ]
    share_c[0].start()
    cold_out[g_rows(core, y), :] = final[...]

    for c in w_over_y:
        c.wait()
    w_over_x = []
    for k in range(1, NX):
        w_over_x.append(
            remote(gath_y, gath_x.at[x], wx_send.at[k - 1], wx_recv.at[k - 1], x_peer(k))
        )
        w_over_x[-1].start()
    gath_x[x] = gath_y[...]

    for k in range(1, NY):
        share_y[k - 1].wait_recv()
        j = lax.rem(y - k + NY, NY)
        rows = cold_out.at[g_rows(core, j)]
        share_c.append(remote(rows, rows, b_send.at[k], b_recv.at[k], sibling))
        share_c[-1].start()

    for c in w_over_x:
        c.wait()
    w_over_c = remote(gath_x, w_out.at[core], wc_sem.at[0], wc_sem.at[1], sibling)
    w_over_c.start()
    w_out[core] = gath_x[...]

    for k in range(1, N_ROW):
        asks[k].wait_send()
        sends[k].wait_send()
        remote(
            stage.at[k], rows_any.at[me], row_send.at[k], row_recv.at[k], (rep, to(k))
        ).wait_send()
    for c in to_core + over_y + share_y:
        c.wait_send()
    for c in share_c:
        c.wait()
    w_over_c.wait()


def step(requests, cold_bags, hot_bags, bottom_weight, table, dense, upstream, top_weight, hot):
    dma = pltpu.SemaphoreType.DMA
    hbm = pl.BlockSpec(memory_space=pl.ANY)
    v = pltpu.VMEM
    rows = (N_ROW, CAP, E)
    return pl.pallas_call(
        step_kernel,
        out_shape=(
            jax.ShapeDtypeStruct((ROWS_DEV, E), BF),
            jax.ShapeDtypeStruct((NC, NX, NY, W_Y, E), BF),
            jax.ShapeDtypeStruct(rows, BF),
            jax.ShapeDtypeStruct(rows, BF),
        ),
        in_specs=[vmem()] * 4 + [hbm] * 5,
        out_specs=(vmem(), vmem(), hbm, hbm),
        scratch_shapes=[
            v((N_ROW, 1, 128), jnp.int32),
            v((N_ROW, 1, 128), jnp.int32),
            pltpu.SMEM((N_ROW, 1, 128), jnp.int32),
            v((ROWS_DEV, E), BF),
            v((ROWS_DEV, E), F32),
            v((CAP, E), F32),
            v(rows, BF),
            v(rows, BF),
            v((B_DEV, D_BOT), BF),
            v((B_DEV, H_TOP), BF),
            v((3 * E, H_TOP), BF),
            v((HOT, E), BF),
            v((SLOTS, B_DEV), BF),
            v((HOT, B_DEV), BF),
            v((B_DEV, 3 * E), BF),
            v((3 * E, B_DEV), BF),
            v((B_DEV, H_TOP), BF),
            v((B_DEV, 3 * E), F32),
            v(rows, BF),
            v((W_ROWS, E), BF),
            v((2, 4, CAP, E), BF),
            v((ROWS_DEV, E), F32),
            v((ROWS_DEV, E), BF),
            v((W_C, E), BF),
            v((W_C, E), BF),
            v((NX - 1, W_X, E), BF),
            v((W_X, E), BF),
            v((NY - 1, W_Y, E), BF),
            v((NZ * W_Z, E), F32),
            v((NZ - 1, W_Z, E), F32),
            v((W_Z, E), F32),
            v((NY, G_Y, E), BF),
            v((NY - 1, G_Y, E), BF),
            v((NY - 1, G_Y, E), BF),
            v((G_Y, E), BF),
            v((NZ, W_Z, E), F32),
            v((NZ * W_Z, E), F32),
            v((NY, W_Y, E), BF),
            v((NX, NY, W_Y, E), BF),
            dma((5,)),
        ]
        + [dma((N_ROW,))] * 6
        + [dma((2,)), dma((2,))]
        + [dma((NX - 1,))] * 2
        + [dma((NY - 1,))] * 2
        + [dma((NZ - 1,))] * 2
        + [dma((NY,))] * 2
        + [dma((NY - 1,))] * 4
        + [dma((NY,))] * 2
        + [dma((NZ - 1,))] * 2
        + [dma((NY - 1,))] * 2
        + [dma((NX - 1,))] * 2
        + [dma((2,))],
        compiler_params=pltpu.CompilerParams(
            collective_id=0, has_side_effects=True, vmem_limit_bytes=VMEM_LIMIT
        ),
        name="step",
    )(requests, cold_bags, hot_bags, bottom_weight, table, dense, upstream, top_weight, hot)


def widen_kernel(cold_ref, w_ref, top_out, bottom_out, hot_out, cold_out):
    for j in range(H_TOP // E):
        top_out[:, j * E : (j + 1) * E] = w_ref[j * 3 * E : (j + 1) * 3 * E, :].astype(F32)
    bottom_out[...] = w_ref[W_BOTTOM:W_HOT, :].astype(F32)
    hot_out[...] = w_ref[W_HOT:W_USED, :].astype(F32)
    cold_out[...] = cold_ref[...].astype(F32)


def widen(cold, w):
    return pl.pallas_call(
        widen_kernel,
        out_shape=(
            jax.ShapeDtypeStruct((3 * E, H_TOP), F32),
            jax.ShapeDtypeStruct((D_BOT, E), F32),
            jax.ShapeDtypeStruct((HOT, E), F32),
            jax.ShapeDtypeStruct((ROWS_DEV, E), F32),
        ),
        in_specs=[vmem()] * 2,
        out_specs=(vmem(),) * 4,
        compiler_params=pltpu.CompilerParams(vmem_limit_bytes=VMEM_LIMIT),
        name="widen",
    )(cold, w)


def local(
    dense_act,
    upstream,
    bottom_weight,
    top_weight,
    hot_table,
    cold_table,
    hot_bags,
    cold_bags,
    requests,
):
    cold, w, _, _ = step(
        requests.reshape(N_ROW, 1, CAP), cold_bags.T, hot_bags.T, bottom_weight, cold_table,
        dense_act, upstream, top_weight, hot_table,
    )
    return widen(cold, w.reshape(W_ROWS, E))


def solution(mesh):
    placed = (
        P(("rep", "row"), None),
        P(("rep", "row"), None),
        P(),
        P(),
        P(),
        P("row", None),
        P(("rep", "row"), None),
        P(("rep", "row"), None),
        P("rep", "row", None, None),
    )
    return jax.shard_map(
        local,
        mesh=mesh,
        in_specs=placed,
        out_specs=(P(), P(), P(), P("row", None)),
        check_vma=False,
    )
```

time: 835 us -> 143 us (0.17)
  waiting for transfers between devices: 605 us -> 0 us
  Pallas kernels: 0 us -> 142 us
  other arithmetic: 94.4 us -> 0 us
  local copies, waits for them, and re-layouts: 65.1 us -> 0 us
  blocking collectives: 30 us -> 0 us
  starting transfers between devices: 16.6 us -> 0 us
  between operations: 14.3 us -> 0.64 us
  matrix products: 9.65 us -> 0 us
    psum x2 -> x0, waiting for transfers between devices: 592 us -> none  [the longest x1 469 us: local(): lax.psum((top_local, bottom_local, hot_local), ('rep', 'row'))]
    pallas_call x0 -> x2, Pallas kernels: none -> 142 us  [the longest x1 138 us: step(): pl.pallas_call(step_kernel, out_shape=(jax.ShapeDtypeStruct((ROWS_DEV, E)...]
    scatter-add x3 -> x0, other arithmetic: 85.5 us -> none  [the longest x1 44.7 us: local(): jax.ops.segment_sum(cold_terms, cold_bags.reshape(-1), num_segments=row_c...]
    gather x3 -> x0, local copies, waits for them, and re-layouts: 53.2 us -> none  [the longest x1 29.5 us: local(): cold_pool = jnp.sum(fetched[cold_bags].astype(jnp.float32), axis=1)]
    all_to_all x1 -> x0, blocking collectives: 30 us -> none  [local(): lax.all_to_all(asked, 'row', split_axis=0, concat_axis=0, tiled=True)]
    all_to_all x2 -> x0, starting transfers between devices: 16.3 us -> none  [the longest x1 11.6 us: local(): lax.all_to_all(slot_grad, 'row', split_axis=0, concat_axis=0, tiled=True)]
    all_to_all x2 -> x0, waiting for transfers between devices: 12.8 us -> none  [the longest x1 12.8 us: local(): lax.all_to_all(gathered, 'row', split_axis=0, concat_axis=0, tiled=True)]
    dot_general x5 -> x0, matrix products: 9.65 us -> none  [the longest x1 2.63 us: local(): jnp.dot(features.T, top_delta, preferred_element_type=jnp.float32)]
  transfers between devices with their start and end apart: 4 -> 0, of which waited for: 3 -> 0; matrix products, arithmetic and copies ran while one was open for 8% -> 0% of each run, Pallas kernels for 0% -> 0%
where the time goes in v2:
time: 143 us
  Pallas kernels  142 us (99%)
    pallas_call x1, Pallas kernels, step(): pl.pallas_call(step_kernel, out_shape=(jax.ShapeDtypeStruct((ROWS_DEV, E)...  138 us
    pallas_call x1, Pallas kernels, widen(): pl.pallas_call(widen_kernel, out_shape=(jax.ShapeDtypeStruct((3 * E, H_TO...  3.67 us

profile of v2, /device:TPU:1, one launch (start us, length us, event | category | flops | bytes accessed | tf_op | source)
XLA Modules:
  0.0 142.8 jit_solution(5687999195255783656)
XLA Ops:
  0.6 138.5 %step.1 = (bf16[4096,128]{1,0:T(8,128)(2,1)}, bf16[2,4,8,64,128]{4,3,2,1,0:T(8,128)(2,1)}, bf16[48,64,128]{2,1,0:T(8,128)(2,1)}, bf16[48,64,128]{2,1,0:T(8,128)(2,1)}) custom-call(s32[48,1,64]{2,1,0:T(1,128)} %bitcast.6, s32[16,512]{1,0:T(8,128)} %bitcast.5, s32[8,512]{1,0:T(8,128)} %bitcast.7, bf16[256,128]{1,0:T(8,128)(2,1)} %bw_ref.1, ...), custom_call_target="tpu_custom_call" | custom-call | tf_op jit(solution)/shard_map/step/pallas_call | solution.py:514
  139.1 3.7 %widen.1 = (f32[384,1024]{1,0:T(8,128)}, f32[256,128]{1,0:T(8,128)}, f32[512,128]{1,0:T(8,128)}, f32[4096,128]{1,0:T(8,128)}) custom-call(bf16[4096,128]{1,0:T(8,128)(2,1)} %get-tuple-element.6.cold_ref, bf16[4096,128]{1,0:T(8,128)(2,1)} %bitcast.4), custom_call_target="tpu_custom_call" | custom-call | tf_op jit(solution)/shard_map/widen/pallas_call | solution.py:594

commit v3 on v2

--- a/solution.py
+++ b/solution.py
@@ -94,11 +94,11 @@
     cold_out, w_out, rows_any, arr_any,
     req_pad, ids_v, ids_smem, table, table32, stage32, stage, fetched,
     dense_ref, up_ref, tw_ref, hott_ref, cold_counts, hot_counts, feats, feats_t, deltas, fgrad,
-    slot, w_ref, arr_v, acc, cold_b,
+    slot, w_ref, arr_v, wanted, hits, give_c,
     part_c, half, part_x, quarter, part_y, eighth, part_z, summed,
     got_c, mine, got_y, final, gath_z, w_y, gath_y, gath_x,
-    load_sem, req_send, req_recv, row_send, row_recv, arr_send, arr_recv, arr_sem,
-    wc, rx_send, rx_recv, ry_send, ry_recv, rz_send, rz_recv,
+    load_sem, req_send, req_recv, row_send, row_recv, arr_send, arr_recv,
+    arr_sem, wc, rx_send, rx_recv, ry_send, ry_recv, rz_send, rz_recv,
     c_send, c_recv, y_send, y_recv, a_send, a_recv, b_send, b_recv,
     wz_send, wz_recv, wy_send, wy_recv, wx_send, wx_recv, wc_sem,
 ):
@@ -138,6 +138,15 @@
         signal(barrier, y_peer(k))
     req_pad[:, :, 0:CAP] = req_ref[...]
     req_pad[:, :, CAP:128] = jnp.zeros((N_ROW, 1, 128 - CAP), jnp.int32)
+    loads[0].wait()
+
+    def widen(i, carry):
+        rows = pl.ds(pl.multiple_of(i * 256, 256), 256)
+        table32[rows, :] = table[rows, :].astype(F32)
+        return carry
+
+    lax.fori_loop(0, ROWS_DEV // 256, widen, 0)
+
     pl.semaphore_wait(barrier, N_ROW - 1 + 1 + NY - 1)
 
     asks = [None]
@@ -149,14 +158,31 @@
         asks[-1].start()
     ids_v[0] = req_pad[me]
 
-    loads[0].wait()
-
-    def widen(i, carry):
-        rows = pl.ds(pl.multiple_of(i * 256, 256), 256)
-        table32[rows, :] = table[rows, :].astype(F32)
+    for k in range(1, N_ROW):
+        asks[k].wait_recv()
+    read = pltpu.make_async_copy(ids_v, ids_smem, load_sem.at[0])
+    read.start()
+    read.wait()
+
+    def pick(k):
+        for i in range(CAP):
+            row = ids_smem[k, 0, i]
+            stage32[pl.ds(i, 1), :] = table32[pl.ds(row, 1), :]
+        stage[k] = stage32[...].astype(BF)
+
+    def serve(k, carry):
+        dx, dz = offset_of(k, core)
+        peer = lax.rem(x - dx + NX, NX) * NZ + lax.rem(z - dz + NZ, NZ)
+        pick(k)
+        remote(
+            stage.at[k], rows_any.at[me], row_send.at[k], row_recv.at[k], (rep, peer)
+        ).start()
         return carry
 
-    lax.fori_loop(0, ROWS_DEV // 256, widen, 0)
+    lax.fori_loop(1, N_ROW, serve, 0)
+    pick(0)
+    own = pltpu.make_async_copy(stage.at[0], rows_any.at[me], load_sem.at[0])
+    own.start()
 
     low = lax.broadcasted_iota(jnp.int32, (128, 128), 0)
 
@@ -186,35 +212,25 @@
             hot_counts[f * 128 : (f + 1) * 128, lanes] = slab
         return carry
 
-    lax.fori_loop(0, B_DEV // 256, count, 0)
-
-    for k in range(1, N_ROW):
-        asks[k].wait_recv()
-    read = pltpu.make_async_copy(ids_v, ids_smem, load_sem.at[0])
-    read.start()
-    read.wait()
-
-    def pick(k):
-        for i in range(CAP):
-            row = ids_smem[k, 0, i]
-            stage32[pl.ds(i, 1), :] = table32[pl.ds(row, 1), :]
-        stage[k] = stage32[...].astype(BF)
-
-    def serve(k, carry):
-        dx, dz = offset_of(k, core)
-        peer = lax.rem(x - dx + NX, NX) * NZ + lax.rem(z - dz + NZ, NZ)
-        pick(k)
-        remote(
-            stage.at[k], rows_any.at[me], row_send.at[k], row_recv.at[k], (rep, peer)
-        ).start()
+    lax.fori_loop(0, B_DEV // 128, count, 0)
+
+    lane = lax.broadcasted_iota(jnp.int32, (1, 128), 1)
+    for j in range(N_ROW // 2):
+        wanted[:, 128 * j : 128 * j + 128] = jnp.where(
+            lane < CAP, ids_v[2 * j], pltpu.roll(ids_v[2 * j + 1], CAP, 1)
+        )
+    place256 = lax.broadcasted_iota(jnp.int32, (256, 512), 0)
+
+    def mark(i, carry):
+        first = pl.multiple_of(i * 256, 256)
+        for j in range(SLOTS // 512):
+            cols = slice(512 * j, 512 * j + 512)
+            found = jnp.where(place256 == wanted[:, cols] - first, 1.0, 0.0)
+            hits[pl.ds(first, 256), cols] = found.astype(BF)
         return carry
 
-    lax.fori_loop(1, N_ROW, serve, 0)
-    pick(0)
-    own = pltpu.make_async_copy(stage.at[0], rows_any.at[me], load_sem.at[0])
-    own.start()
-
-    lax.fori_loop(B_DEV // 256, B_DEV // 128, count, 0)
+    lax.fori_loop(0, ROWS_DEV // 256, mark, 0)
+
     loads[1].wait()
     bottom_pre = jnp.dot(dense_ref[...], bw_ref[...], preferred_element_type=F32)
     lower = bottom_pre * jax.nn.sigmoid(bottom_pre)
@@ -263,7 +279,13 @@
         sends.append(
             remote(slot.at[peer], arr_any.at[k], arr_send.at[k], arr_recv.at[k], (rep, peer))
         )
-        sends[-1].start()
+
+
+    def issue(first, last):
+        for k in range(first, last):
+            sends[k].start()
+
+    issue(1, 9)
     own = pltpu.make_async_copy(slot.at[me], arr_any.at[0], load_sem.at[0])
     own.start()
 
@@ -286,51 +308,7 @@
         sibling,
     )
     to_half.start()
-
-    lane = lax.broadcasted_iota(jnp.int32, (1, 128), 1)
-    place512 = lax.broadcasted_iota(jnp.int32, (512, 256), 0)
-
-    def arrive(g):
-        for k in range(4 * g, 4 * g + 4):
-            if k == 0:
-                own.wait()
-            else:
-                sends[k].wait_recv()
-        copy = pltpu.make_async_copy(arr_any.at[4 * g : 4 * g + 4], arr_v.at[g % 2], arr_sem.at[g % 2])
-        copy.start()
-        return copy
-
-    def pair(k):
-        return jnp.where(lane < CAP, ids_v[k], pltpu.roll(ids_v[k + 1], CAP, 1))
-
-    def gather_in(g):
-        wanted = jnp.concatenate([pair(4 * g), pair(4 * g + 2)], axis=1)
-        values = arr_v[g % 2].reshape(4 * CAP, E)
-
-        def block(i, carry):
-            first = pl.multiple_of(i * 512, 512)
-            hits = jnp.where(place512 == wanted - first, 1.0, 0.0).astype(BF)
-            term = jnp.dot(hits, values, preferred_element_type=F32)
-            rows = pl.ds(first, 512)
-            if g == 0:
-                acc[rows, :] = term
-            elif g == N_ROW // 4 - 1:
-                cold_b[rows, :] = (acc[rows, :] + term).astype(BF)
-            else:
-                acc[rows, :] += term
-            return carry
-
-        lax.fori_loop(0, ROWS_DEV // 512, block, 0)
-
-    def groups(lo, hi, copy):
-        for g in range(lo, hi):
-            copy.wait()
-            following = arrive(g + 1) if g + 1 < N_ROW // 4 else None
-            gather_in(g)
-            copy = following
-        return copy
-
-    copy = groups(0, 2, arrive(0))
+    issue(9, 15)
 
     to_half.wait()
 
@@ -351,8 +329,7 @@
             )
         )
         to_x[-1].start()
-
-    copy = groups(2, 6, copy)
+    issue(15, 21)
 
     for c in to_x:
         c.wait()
@@ -370,8 +347,7 @@
             )
         )
         to_y[-1].start()
-
-    copy = groups(6, 9, copy)
+    issue(21, 27)
 
     for c in to_y:
         c.wait()
@@ -390,22 +366,7 @@
             )
         )
         to_z[-1].start()
-
-    groups(9, N_ROW // 4, copy)
-
-    def g_rows(c, j):
-        return pl.ds(pl.multiple_of(c * G_C + j * G_Y, G_Y), G_Y)
-
-    to_core = []
-    for k in range(1, NY + 1):
-        j = lax.rem(y + k, NY)
-        to_core.append(
-            remote(
-                cold_b.at[g_rows(1 - core, j)], got_c.at[k - 1], c_send.at[k - 1],
-                c_recv.at[k - 1], sibling,
-            )
-        )
-        to_core[-1].start()
+    issue(27, 33)
 
     for c in to_z:
         c.wait()
@@ -420,20 +381,7 @@
             remote(summed, gath_z.at[k], wz_send.at[k - 1], wz_recv.at[k - 1], z_peer(k))
         )
         over_z[-1].start()
-
-    over_y = []
-    for k in range(1, NY + 1):
-        j = lax.rem(y + k, NY)
-        to_core[k - 1].wait_recv()
-        total = cold_b[g_rows(core, j), :].astype(F32) + got_c[k - 1].astype(F32)
-        if k < NY:
-            mine[k - 1] = total.astype(BF)
-            over_y.append(
-                remote(
-                    mine.at[k - 1], got_y.at[k - 1], y_send.at[k - 1], y_recv.at[k - 1], y_peer(k)
-                )
-            )
-            over_y[-1].start()
+    issue(33, 39)
 
     for c in over_z:
         c.wait()
@@ -451,16 +399,90 @@
             remote(gath_y.at[y], gath_y.at[y], wy_send.at[k - 1], wy_recv.at[k - 1], y_peer(k))
         )
         w_over_y[-1].start()
-
-    for k in range(1, NY):
-        over_y[k - 1].wait_recv()
-        total += got_y[k - 1].astype(F32)
+    issue(39, 44)
+
+    for c in w_over_y:
+        c.wait()
+    w_over_x = []
+    for k in range(1, NX):
+        w_over_x.append(
+            remote(gath_y, gath_x.at[x], wx_send.at[k - 1], wx_recv.at[k - 1], x_peer(k))
+        )
+        w_over_x[-1].start()
+    issue(44, N_ROW)
+    gath_x[x] = gath_y[...]
+
+    copies = []
+    for part in range(4):
+        for k in range(12 * part, 12 * part + 12):
+            if k == 0:
+                own.wait()
+            else:
+                sends[k].wait_recv()
+        chunk = pl.ds(12 * part, 12)
+        copies.append(
+            pltpu.make_async_copy(arr_any.at[chunk], arr_v.at[chunk], arr_sem.at[part])
+        )
+        copies[-1].start()
+    for c in copies:
+        c.wait()
+
+    def g_rows(c, j):
+        return pl.ds(pl.multiple_of(c * G_C + j * G_Y, G_Y), G_Y)
+
+    sign = 1 - 2 * core
+
+    def ring(step):
+        return lax.rem(y + step + NY, NY)
+
+    def ring_peer(step):
+        return (ring(step) * NC + core, me)
+
+    def steps(s):
+        return [4, s, -s, 2 * s, -2 * s, -3 * s, 3 * s, 0]
+
+    def owned(c, j):
+        values = arr_v[...].reshape(SLOTS, E)
+        total = jnp.dot(hits[g_rows(c, j), :], values, preferred_element_type=F32)
+        return total.astype(BF)
+
+    to_core = []
+    for i, step in enumerate(steps(-sign)):
+        give_c[i] = owned(1 - core, ring(step))
+        to_core.append(
+            remote(give_c.at[i], got_c.at[i], c_send.at[i], c_recv.at[i], sibling)
+        )
+        to_core[-1].start()
+
+    over_y = []
+    for i, step in enumerate(steps(sign)):
+        total = owned(core, ring(step)).astype(F32)
+        to_core[i].wait_recv()
+        total += got_c[i].astype(F32)
+        if i == NY - 2:
+            over_y[0].wait_recv()
+            total += got_y[0].astype(F32)
+        if i < NY - 1:
+            mine[i] = total.astype(BF)
+            peer = ring_peer(sign) if i == 0 else ring_peer(step)
+            over_y.append(remote(mine.at[i], got_y.at[i], y_send.at[i], y_recv.at[i], peer))
+            over_y[-1].start()
+
+    for c in w_over_x:
+        c.wait()
+    w_over_c = remote(gath_x, w_out.at[core], wc_sem.at[0], wc_sem.at[1], sibling)
+    w_over_c.start()
+    w_out[core] = gath_x[...]
+
+    for i in range(1, NY - 1):
+        over_y[i].wait_recv()
+        total += got_y[i].astype(F32)
     final[...] = total.astype(BF)
     share_y = []
-    for k in range(1, NY):
+    for i, step in enumerate(steps(sign)[1:7]):
         share_y.append(
             remote(
-                final, cold_out.at[g_rows(core, y)], a_send.at[k - 1], a_recv.at[k - 1], y_peer(k)
+                final, cold_out.at[g_rows(core, y)], a_send.at[i], a_recv.at[i], ring_peer(step)
             )
         )
         share_y[-1].start()
@@ -470,28 +492,21 @@
     share_c[0].start()
     cold_out[g_rows(core, y), :] = final[...]
 
-    for c in w_over_y:
-        c.wait()
-    w_over_x = []
-    for k in range(1, NX):
-        w_over_x.append(
-            remote(gath_y, gath_x.at[x], wx_send.at[k - 1], wx_recv.at[k - 1], x_peer(k))
-        )
-        w_over_x[-1].start()
-    gath_x[x] = gath_y[...]
-
-    for k in range(1, NY):
-        share_y[k - 1].wait_recv()
-        j = lax.rem(y - k + NY, NY)
-        rows = cold_out.at[g_rows(core, j)]
-        share_c.append(remote(rows, rows, b_send.at[k], b_recv.at[k], sibling))
+    def forward(i, step):
+        rows = cold_out.at[g_rows(core, ring(-step))]
+        share_c.append(remote(rows, rows, b_send.at[i], b_recv.at[i], sibling))
         share_c[-1].start()
 
-    for c in w_over_x:
-        c.wait()
-    w_over_c = remote(gath_x, w_out.at[core], wc_sem.at[0], wc_sem.at[1], sibling)
-    w_over_c.start()
-    w_out[core] = gath_x[...]
+    share_y[5].wait_recv()
+    rows = cold_out.at[g_rows(core, ring(-3 * sign))]
+    share_y.append(remote(rows, rows, a_send.at[6], a_recv.at[6], ring_peer(sign)))
+    share_y[6].start()
+    forward(6, 3 * sign)
+    for i, step in enumerate(steps(sign)[1:6]):
+        share_y[i].wait_recv()
+        forward(i + 1, step)
+    share_y[6].wait_recv()
+    forward(7, 4)
 
     for k in range(1, N_ROW):
         asks[k].wait_send()
@@ -542,9 +557,10 @@
             v((B_DEV, 3 * E), F32),
             v(rows, BF),
             v((W_ROWS, E), BF),
-            v((2, 4, CAP, E), BF),
-            v((ROWS_DEV, E), F32),
-            v((ROWS_DEV, E), BF),
+            v(rows, BF),
+            v((1, SLOTS), jnp.int32),
+            v((ROWS_DEV, SLOTS), BF),
+            v((NY, G_Y, E), BF),
             v((W_C, E), BF),
             v((W_C, E), BF),
             v((NX - 1, W_X, E), BF),
@@ -564,7 +580,7 @@
             dma((5,)),
         ]
         + [dma((N_ROW,))] * 6
-        + [dma((2,)), dma((2,))]
+        + [dma((4,)), dma((2,))]
         + [dma((NX - 1,))] * 2
         + [dma((NY - 1,))] * 2
         + [dma((NZ - 1,))] * 2

time: 143 us -> 151 us (1.056)
  Pallas kernels: 142 us -> 150 us
    pallas_call x1, Pallas kernels: 138 us -> 146 us  [step(): pl.pallas_call(step_kernel, out_shape=(jax.ShapeDtypeStruct((ROWS_DEV, E)...]
where the time goes in v3:
time: 151 us; the launch traced here: 150 us
  Pallas kernels  150 us (99%)
    pallas_call x1, Pallas kernels, step(): pl.pallas_call(step_kernel, out_shape=(jax.ShapeDtypeStruct((ROWS_DEV, E)...  146 us
    pallas_call x1, Pallas kernels, widen(): pl.pallas_call(widen_kernel, out_shape=(jax.ShapeDtypeStruct((3 * E, H_TO...  3.67 us

profile of v3, /device:TPU:1, one launch (start us, length us, event | category | flops | bytes accessed | tf_op | source)
XLA Modules:
  0.0 150.3 jit_solution(5927731758278711146)
XLA Ops:
  0.6 146.0 %step.1 = (bf16[4096,128]{1,0:T(8,128)(2,1)}, bf16[2,4,8,64,128]{4,3,2,1,0:T(8,128)(2,1)}, bf16[48,64,128]{2,1,0:T(8,128)(2,1)}, bf16[48,64,128]{2,1,0:T(8,128)(2,1)}) custom-call(s32[48,1,64]{2,1,0:T(1,128)} %bitcast.6, s32[16,512]{1,0:T(8,128)} %bitcast.5, s32[8,512]{1,0:T(8,128)} %bitcast.7, bf16[256,128]{1,0:T(8,128)(2,1)} %bw_ref.1, ...), custom_call_target="tpu_custom_call" | custom-call | tf_op jit(solution)/shard_map/step/pallas_call | solution.py:529
  146.6 3.7 %widen.1 = (f32[384,1024]{1,0:T(8,128)}, f32[256,128]{1,0:T(8,128)}, f32[512,128]{1,0:T(8,128)}, f32[4096,128]{1,0:T(8,128)}) custom-call(bf16[4096,128]{1,0:T(8,128)(2,1)} %get-tuple-element.6.cold_ref, bf16[4096,128]{1,0:T(8,128)(2,1)} %bitcast.4), custom_call_target="tpu_custom_call" | custom-call | tf_op jit(solution)/shard_map/widen/pallas_call | solution.py:610

commit v4 on v3

--- a/solution.py
+++ b/solution.py
@@ -24,8 +24,8 @@
 W_USED = W_HOT + HOT
 W_ROWS = 4096
 W_C = W_ROWS // NC
-W_X = W_C // NX
-W_Y = W_X // NY
+W_Y = W_C // NY
+W_X = W_Y // NX
 W_Z = 8
 
 G_C = ROWS_DEV // NC
@@ -96,7 +96,7 @@
     dense_ref, up_ref, tw_ref, hott_ref, cold_counts, hot_counts, feats, feats_t, deltas, fgrad,
     slot, w_ref, arr_v, wanted, hits, give_c,
     part_c, half, part_x, quarter, part_y, eighth, part_z, summed,
-    got_c, mine, got_y, final, gath_z, w_y, gath_y, gath_x,
+    got_c, mine, got_y, final, gath_z, w_x, gath_x, gath_y,
     load_sem, req_send, req_recv, row_send, row_recv, arr_send, arr_recv,
     arr_sem, wc, rx_send, rx_recv, ry_send, ry_recv, rz_send, rz_recv,
     c_send, c_recv, y_send, y_recv, a_send, a_recv, b_send, b_recv,
@@ -273,22 +273,6 @@
         )
         slot[8 * s : 8 * s + 8] = total.astype(BF).reshape(8, CAP, E)
 
-    sends = [None]
-    for k in range(1, N_ROW):
-        peer = to(k)
-        sends.append(
-            remote(slot.at[peer], arr_any.at[k], arr_send.at[k], arr_recv.at[k], (rep, peer))
-        )
-
-
-    def issue(first, last):
-        for k in range(first, last):
-            sends[k].start()
-
-    issue(1, 9)
-    own = pltpu.make_async_copy(slot.at[me], arr_any.at[0], load_sem.at[0])
-    own.start()
-
     feats_t[...] = feats[...].astype(F32).T.astype(BF)
     for h in range(H_TOP // 256):
         cols = slice(h * 256, (h + 1) * 256)
@@ -308,7 +292,17 @@
         sibling,
     )
     to_half.start()
-    issue(9, 15)
+
+    sends = [None]
+    for k in range(1, N_ROW):
+        peer = to(k)
+        sends.append(
+            remote(slot.at[peer], arr_any.at[k], arr_send.at[k], arr_recv.at[k], (rep, peer))
+        )
+
+        sends[-1].start()
+    own = pltpu.make_async_copy(slot.at[me], arr_any.at[0], load_sem.at[0])
+    own.start()
 
     to_half.wait()
 
@@ -319,98 +313,32 @@
         return carry
 
     lax.fori_loop(0, W_C // 256, add_c, 0)
+    to_y = []
+    for k in range(1, NY):
+        py = lax.rem(y + k, NY)
+        to_y.append(
+            remote(
+                half.at[pl.ds(pl.multiple_of(py * W_Y, W_Y), W_Y)], part_y.at[k - 1],
+                ry_send.at[k - 1], ry_recv.at[k - 1], y_peer(k),
+            )
+        )
+        to_y[-1].start()
+    for c in to_y:
+        c.wait()
+    total = half[pl.ds(pl.multiple_of(y * W_Y, W_Y), W_Y), :].astype(F32)
+    for k in range(1, NY):
+        total += part_y[k - 1].astype(F32)
+    quarter[...] = total.astype(BF)
     to_x = []
     for k in range(1, NX):
         px = lax.rem(x + k, NX)
         to_x.append(
             remote(
-                half.at[pl.ds(pl.multiple_of(px * W_X, W_X), W_X)], part_x.at[k - 1],
+                quarter.at[pl.ds(pl.multiple_of(px * W_X, W_X), W_X)], part_x.at[k - 1],
                 rx_send.at[k - 1], rx_recv.at[k - 1], x_peer(k),
             )
         )
         to_x[-1].start()
-    issue(15, 21)
-
-    for c in to_x:
-        c.wait()
-    total = half[pl.ds(pl.multiple_of(x * W_X, W_X), W_X), :].astype(F32)
-    for k in range(1, NX):
-        total += part_x[k - 1].astype(F32)
-    quarter[...] = total.astype(BF)
-    to_y = []
-    for k in range(1, NY):
-        py = lax.rem(y + k, NY)
-        to_y.append(
-            remote(
-                quarter.at[pl.ds(pl.multiple_of(py * W_Y, W_Y), W_Y)], part_y.at[k - 1],
-                ry_send.at[k - 1], ry_recv.at[k - 1], y_peer(k),
-            )
-        )
-        to_y[-1].start()
-    issue(21, 27)
-
-    for c in to_y:
-        c.wait()
-    total = quarter[pl.ds(pl.multiple_of(y * W_Y, W_Y), W_Y), :].astype(F32)
-    for k in range(1, NY):
-        total += part_y[k - 1].astype(F32)
-    eighth[0:W_Y, :] = total
-    eighth[W_Y : NZ * W_Z, :] = jnp.zeros((NZ * W_Z - W_Y, E), F32)
-    to_z = []
-    for k in range(1, NZ):
-        pz = lax.rem(z + k, NZ)
-        to_z.append(
-            remote(
-                eighth.at[pl.ds(pl.multiple_of(pz * W_Z, W_Z), W_Z)], part_z.at[k - 1],
-                rz_send.at[k - 1], rz_recv.at[k - 1], z_peer(k),
-            )
-        )
-        to_z[-1].start()
-    issue(27, 33)
-
-    for c in to_z:
-        c.wait()
-    total = eighth[pl.ds(pl.multiple_of(z * W_Z, W_Z), W_Z), :]
-    for k in range(1, NZ):
-        total += part_z[k - 1]
-    summed[...] = total
-    gath_z[0] = total
-    over_z = []
-    for k in range(1, NZ):
-        over_z.append(
-            remote(summed, gath_z.at[k], wz_send.at[k - 1], wz_recv.at[k - 1], z_peer(k))
-        )
-        over_z[-1].start()
-    issue(33, 39)
-
-    for c in over_z:
-        c.wait()
-
-    def place(k, carry):
-        owner_z = lax.rem(z - k + NZ, NZ)
-        w_y[pl.ds(pl.multiple_of(owner_z * W_Z, W_Z), W_Z), :] = gath_z[k]
-        return carry
-
-    lax.fori_loop(0, NZ, place, 0)
-    gath_y[y] = w_y[0:W_Y, :].astype(BF)
-    w_over_y = []
-    for k in range(1, NY):
-        w_over_y.append(
-            remote(gath_y.at[y], gath_y.at[y], wy_send.at[k - 1], wy_recv.at[k - 1], y_peer(k))
-        )
-        w_over_y[-1].start()
-    issue(39, 44)
-
-    for c in w_over_y:
-        c.wait()
-    w_over_x = []
-    for k in range(1, NX):
-        w_over_x.append(
-            remote(gath_y, gath_x.at[x], wx_send.at[k - 1], wx_recv.at[k - 1], x_peer(k))
-        )
-        w_over_x[-1].start()
-    issue(44, N_ROW)
-    gath_x[x] = gath_y[...]
 
     copies = []
     for part in range(4):
@@ -446,6 +374,43 @@
         total = jnp.dot(hits[g_rows(c, j), :], values, preferred_element_type=F32)
         return total.astype(BF)
 
+    def add_x():
+        for c in to_x:
+            c.wait()
+        total = quarter[pl.ds(pl.multiple_of(x * W_X, W_X), W_X), :].astype(F32)
+        for k in range(1, NX):
+            total += part_x[k - 1].astype(F32)
+        eighth[0:W_X, :] = total
+        eighth[W_X : NZ * W_Z, :] = jnp.zeros((NZ * W_Z - W_X, E), F32)
+        copies = []
+        for k in range(1, NZ):
+            pz = lax.rem(z + k, NZ)
+            copies.append(
+                remote(
+                    eighth.at[pl.ds(pl.multiple_of(pz * W_Z, W_Z), W_Z)], part_z.at[k - 1],
+                    rz_send.at[k - 1], rz_recv.at[k - 1], z_peer(k),
+                )
+            )
+            copies[-1].start()
+        return copies
+
+    def add_z():
+        for c in to_z:
+            c.wait()
+        total = eighth[pl.ds(pl.multiple_of(z * W_Z, W_Z), W_Z), :]
+        for k in range(1, NZ):
+            total += part_z[k - 1]
+        summed[...] = total
+        gath_z[0] = total
+        copies = []
+        for k in range(1, NZ):
+            copies.append(
+                remote(summed, gath_z.at[k], wz_send.at[k - 1], wz_recv.at[k - 1], z_peer(k))
+            )
+            copies[-1].start()
+        return copies
+
+    to_z = add_x()
     to_core = []
     for i, step in enumerate(steps(-sign)):
         give_c[i] = owned(1 - core, ring(step))
@@ -453,6 +418,7 @@
             remote(give_c.at[i], got_c.at[i], c_send.at[i], c_recv.at[i], sibling)
         )
         to_core[-1].start()
+    over_z = add_z()
 
     over_y = []
     for i, step in enumerate(steps(sign)):
@@ -468,11 +434,22 @@
             over_y.append(remote(mine.at[i], got_y.at[i], y_send.at[i], y_recv.at[i], peer))
             over_y[-1].start()
 
-    for c in w_over_x:
+    for c in over_z:
         c.wait()
-    w_over_c = remote(gath_x, w_out.at[core], wc_sem.at[0], wc_sem.at[1], sibling)
-    w_over_c.start()
-    w_out[core] = gath_x[...]
+
+    def place(k, carry):
+        owner_z = lax.rem(z - k + NZ, NZ)
+        w_x[pl.ds(pl.multiple_of(owner_z * W_Z, W_Z), W_Z), :] = gath_z[k]
+        return carry
+
+    lax.fori_loop(0, NZ, place, 0)
+    gath_y[y] = w_x[0:W_X, :].astype(BF)
+    w_over_y = []
+    for k in range(1, NY):
+        w_over_y.append(
+            remote(gath_y.at[y], gath_y.at[y], wy_send.at[k - 1], wy_recv.at[k - 1], y_peer(k))
+        )
+        w_over_y[-1].start()
 
     for i in range(1, NY - 1):
         over_y[i].wait_recv()
@@ -497,6 +474,16 @@
         share_c.append(remote(rows, rows, b_send.at[i], b_recv.at[i], sibling))
         share_c[-1].start()
 
+    for c in w_over_y:
+        c.wait()
+    w_over_x = []
+    for k in range(1, NX):
+        w_over_x.append(
+            remote(gath_y, gath_x.at[x], wx_send.at[k - 1], wx_recv.at[k - 1], x_peer(k))
+        )
+        w_over_x[-1].start()
+    gath_x[x] = gath_y[...]
+
     share_y[5].wait_recv()
     rows = cold_out.at[g_rows(core, ring(-3 * sign))]
     share_y.append(remote(rows, rows, a_send.at[6], a_recv.at[6], ring_peer(sign)))
@@ -505,6 +492,11 @@
     for i, step in enumerate(steps(sign)[1:6]):
         share_y[i].wait_recv()
         forward(i + 1, step)
+    for c in w_over_x:
+        c.wait()
+    w_over_c = remote(gath_x, w_out.at[core], wc_sem.at[0], wc_sem.at[1], sibling)
+    w_over_c.start()
+    w_out[core] = gath_x[...]
     share_y[6].wait_recv()
     forward(7, 4)
 
@@ -530,7 +522,7 @@
         step_kernel,
         out_shape=(
             jax.ShapeDtypeStruct((ROWS_DEV, E), BF),
-            jax.ShapeDtypeStruct((NC, NX, NY, W_Y, E), BF),
+            jax.ShapeDtypeStruct((NC, NX, NY, W_X, E), BF),
             jax.ShapeDtypeStruct(rows, BF),
             jax.ShapeDtypeStruct(rows, BF),
         ),
@@ -564,7 +556,7 @@
             v((W_C, E), BF),
             v((W_C, E), BF),
             v((NX - 1, W_X, E), BF),
-            v((W_X, E), BF),
+            v((W_Y, E), BF),
             v((NY - 1, W_Y, E), BF),
             v((NZ * W_Z, E), F32),
             v((NZ - 1, W_Z, E), F32),
@@ -575,8 +567,8 @@
             v((G_Y, E), BF),
             v((NZ, W_Z, E), F32),
             v((NZ * W_Z, E), F32),
-            v((NY, W_Y, E), BF),
-            v((NX, NY, W_Y, E), BF),
+            v((NX, NY, W_X, E), BF),
+            v((NY, W_X, E), BF),
             dma((5,)),
         ]
         + [dma((N_ROW,))] * 6
@@ -599,10 +591,18 @@
 
 
 def widen_kernel(cold_ref, w_ref, top_out, bottom_out, hot_out, cold_out):
-    for j in range(H_TOP // E):
-        top_out[:, j * E : (j + 1) * E] = w_ref[j * 3 * E : (j + 1) * 3 * E, :].astype(F32)
-    bottom_out[...] = w_ref[W_BOTTOM:W_HOT, :].astype(F32)
-    hot_out[...] = w_ref[W_HOT:W_USED, :].astype(F32)
+    for c in range(NC):
+        for yy in range(NY):
+            for xx in range(NX):
+                row = c * W_C + yy * W_Y + xx * W_X
+                values = w_ref[c, xx, yy].astype(F32)
+                if row < W_BOTTOM:
+                    col, first = row // (3 * E), row % (3 * E)
+                    top_out[first : first + W_X, col * E : (col + 1) * E] = values
+                elif row < W_HOT:
+                    bottom_out[row - W_BOTTOM : row - W_BOTTOM + W_X, :] = values
+                elif row < W_USED:
+                    hot_out[row - W_HOT : row - W_HOT + W_X, :] = values
     cold_out[...] = cold_ref[...].astype(F32)
 
 
@@ -637,7 +637,7 @@
         requests.reshape(N_ROW, 1, CAP), cold_bags.T, hot_bags.T, bottom_weight, cold_table,
         dense_act, upstream, top_weight, hot_table,
     )
-    return widen(cold, w.reshape(W_ROWS, E))
+    return widen(cold, w)
 
 
 def solution(mesh):

time: 151 us -> 133 us (0.88)
  Pallas kernels: 150 us -> 131 us
    pallas_call x1, Pallas kernels: 146 us -> 128 us  [step(): pl.pallas_call(step_kernel, out_shape=(jax.ShapeDtypeStruct((ROWS_DEV, E)...]
where the time goes in v4:
time: 133 us; the launch traced here: 132 us
  Pallas kernels  131 us (98%)
    pallas_call x1, Pallas kernels, step(): pl.pallas_call(step_kernel, out_shape=(jax.ShapeDtypeStruct((ROWS_DEV, E)...  128 us
    pallas_call x1, Pallas kernels, widen(): pl.pallas_call(widen_kernel, out_shape=(jax.ShapeDtypeStruct((3 * E, H_TO...  3.67 us

profile of v4, /device:TPU:1, one launch (start us, length us, event | category | flops | bytes accessed | tf_op | source)
XLA Modules:
  0.0 131.8 jit_solution(2081772548650239185)
XLA Ops:
  0.6 127.5 %step.1 = (bf16[4096,128]{1,0:T(8,128)(2,1)}, bf16[2,4,8,64,128]{4,3,2,1,0:T(8,128)(2,1)}, bf16[48,64,128]{2,1,0:T(8,128)(2,1)}, bf16[48,64,128]{2,1,0:T(8,128)(2,1)}) custom-call(s32[48,1,64]{2,1,0:T(1,128)} %bitcast.4, s32[16,512]{1,0:T(8,128)} %bitcast.3, s32[8,512]{1,0:T(8,128)} %bitcast.5, bf16[256,128]{1,0:T(8,128)(2,1)} %bw_ref.1, ...), custom_call_target="tpu_custom_call" | custom-call | tf_op jit(solution)/shard_map/step/pallas_call | solution.py:521
  128.2 3.7 %widen.1 = (f32[384,1024]{1,0:T(8,128)}, f32[256,128]{1,0:T(8,128)}, f32[512,128]{1,0:T(8,128)}, f32[4096,128]{1,0:T(8,128)}) custom-call(bf16[4096,128]{1,0:T(8,128)(2,1)} %get-tuple-element.6.cold_ref, bf16[2,4,8,64,128]{4,3,2,1,0:T(8,128)(2,1)} %get-tuple-element.7.w_ref), custom_call_target="tpu_custom_call" | custom-call | tf_op jit(solution)/shard_map/widen/pallas_call | solution.py:610

commit v5 on v4

--- a/solution.py
+++ b/solution.py
@@ -170,7 +170,8 @@
             stage32[pl.ds(i, 1), :] = table32[pl.ds(row, 1), :]
         stage[k] = stage32[...].astype(BF)
 
-    def serve(k, carry):
+    def serve(i, carry):
+        k = N_ROW - i
         dx, dz = offset_of(k, core)
         peer = lax.rem(x - dx + NX, NX) * NZ + lax.rem(z - dz + NZ, NZ)
         pick(k)
@@ -412,16 +413,22 @@
 
     to_z = add_x()
     to_core = []
-    for i, step in enumerate(steps(-sign)):
-        give_c[i] = owned(1 - core, ring(step))
+
+    def give(i):
+        give_c[i] = owned(1 - core, ring(steps(-sign)[i]))
         to_core.append(
             remote(give_c.at[i], got_c.at[i], c_send.at[i], c_recv.at[i], sibling)
         )
         to_core[-1].start()
-    over_z = add_z()
-
+
+    give(0)
+    give(1)
     over_y = []
     for i, step in enumerate(steps(sign)):
+        if i + 2 < NY:
+            give(i + 2)
+        if i == 3:
+            over_z = add_z()
         total = owned(core, ring(step)).astype(F32)
         to_core[i].wait_recv()
         total += got_c[i].astype(F32)
@@ -456,7 +463,8 @@
         total += got_y[i].astype(F32)
     final[...] = total.astype(BF)
     share_y = []
-    for i, step in enumerate(steps(sign)[1:7]):
+    onward = [3 * sign, sign, -sign, 2 * sign, -2 * sign, -3 * sign]
+    for i, step in enumerate(onward):
         share_y.append(
             remote(
                 final, cold_out.at[g_rows(core, y)], a_send.at[i], a_recv.at[i], ring_peer(step)
@@ -484,13 +492,13 @@
         w_over_x[-1].start()
     gath_x[x] = gath_y[...]
 
-    share_y[5].wait_recv()
+    share_y[0].wait_recv()
     rows = cold_out.at[g_rows(core, ring(-3 * sign))]
     share_y.append(remote(rows, rows, a_send.at[6], a_recv.at[6], ring_peer(sign)))
     share_y[6].start()
-    forward(6, 3 * sign)
-    for i, step in enumerate(steps(sign)[1:6]):
-        share_y[i].wait_recv()
+    for i, step in enumerate(onward):
+        if i > 0:
+            share_y[i].wait_recv()
         forward(i + 1, step)
     for c in w_over_x:
         c.wait()

time: 133 us -> 137 us (1.030)
  Pallas kernels: 131 us -> 136 us
    pallas_call x1, Pallas kernels: 128 us -> 133 us  [step(): pl.pallas_call(step_kernel, out_shape=(jax.ShapeDtypeStruct((ROWS_DEV, E)...]
where the time goes in v5:
time: 137 us
  Pallas kernels  136 us (99%)
    pallas_call x1, Pallas kernels, step(): pl.pallas_call(step_kernel, out_shape=(jax.ShapeDtypeStruct((ROWS_DEV, E)...  133 us
    pallas_call x1, Pallas kernels, widen(): pl.pallas_call(widen_kernel, out_shape=(jax.ShapeDtypeStruct((3 * E, H_TO...  3.67 us

profile of v5, /device:TPU:1, one launch (start us, length us, event | category | flops | bytes accessed | tf_op | source)
XLA Modules:
  0.0 137.0 jit_solution(15012161599911476348)
XLA Ops:
  0.6 132.7 %step.1 = (bf16[4096,128]{1,0:T(8,128)(2,1)}, bf16[2,4,8,64,128]{4,3,2,1,0:T(8,128)(2,1)}, bf16[48,64,128]{2,1,0:T(8,128)(2,1)}, bf16[48,64,128]{2,1,0:T(8,128)(2,1)}) custom-call(s32[48,1,64]{2,1,0:T(1,128)} %bitcast.4, s32[16,512]{1,0:T(8,128)} %bitcast.3, s32[8,512]{1,0:T(8,128)} %bitcast.5, bf16[256,128]{1,0:T(8,128)(2,1)} %bw_ref.1, ...), custom_call_target="tpu_custom_call" | custom-call | tf_op jit(solution)/shard_map/step/pallas_call | solution.py:529
  133.3 3.7 %widen.1 = (f32[384,1024]{1,0:T(8,128)}, f32[256,128]{1,0:T(8,128)}, f32[512,128]{1,0:T(8,128)}, f32[4096,128]{1,0:T(8,128)}) custom-call(bf16[4096,128]{1,0:T(8,128)(2,1)} %get-tuple-element.6.cold_ref, bf16[2,4,8,64,128]{4,3,2,1,0:T(8,128)(2,1)} %get-tuple-element.7.w_ref), custom_call_target="tpu_custom_call" | custom-call | tf_op jit(solution)/shard_map/widen/pallas_call | solution.py:618
